TPU v7x, 256 devices: a whole 4x4x8 slice. The times are simulated.
256 devices in a mesh: row: 16 (over z, y_lo), col: 16 (over y_hi, x, core).
Axes of the slice: x: 4, y: 4 (y_hi: 2, y_lo: 2; y = y_hi * 2 + y_lo), z: 8, core: 2. Of those that a mesh axis runs over, the one named last changes fastest.
Arguments:
- pair_map: bfloat16 [768, 768, 128], P('row', 'col'), may hold values from -6 to 6
- saved_product: bfloat16 [768, 768, 128], P('row', 'col'), may hold values from -6 to 6
- cotangent: bfloat16 [768, 768, 128], P('row', 'col'), may hold values from -1.5 to 1.5
- residue_mask: int32 [768], replicated, may hold values from 0 to 1, as said below
- ln_gain: float32 [128], replicated, may hold values from 0.25 to 1.75
- ln_bias: float32 [128], replicated, may hold values from -0.5 to 0.5
- out_gain: float32 [128], replicated, may hold values from 0.25 to 1.75
- out_bias: float32 [128], replicated, may hold values from -0.5 to 0.5
- w_a: bfloat16 [128, 128], replicated, may hold values from -0.5 to 0.5
- w_ag: bfloat16 [128, 128], replicated, may hold values from -0.5 to 0.5
- w_b: bfloat16 [128, 128], replicated, may hold values from -0.5 to 0.5
- w_bg: bfloat16 [128, 128], replicated, may hold values from -0.5 to 0.5
- w_g: bfloat16 [128, 128], replicated, may hold values from -0.5 to 0.5
- w_o: bfloat16 [128, 128], replicated, may hold values from -0.5 to 0.5
Outputs:
- grad_pair: bfloat16 [768, 768, 128], P('row', 'col')
- grad_w_a: float32 [128, 128], replicated
- grad_w_ag: float32 [128, 128], replicated
- grad_w_b: float32 [128, 128], replicated
- grad_w_bg: float32 [128, 128], replicated
- grad_w_g: float32 [128, 128], replicated
- grad_w_o: float32 [128, 128], replicated
- grad_ln_gain: float32 [128], replicated
- grad_ln_bias: float32 [128], replicated
- grad_out_gain: float32 [128], replicated
- grad_out_bias: float32 [128], replicated
Inputs may be any that keep to these rules, and one draw needn't show every extreme that they name: `residue_mask`: between 1 and 192 residues are 0, anywhere in the crop.
All inputs are finite; a program needn't handle non-finite values.
Results may differ from a plain program's by a relative error of at most 0.02.
Values may be sent and summed in bfloat16 or wider, within the bound.
A program may use at most 128 MiB of HBM per device.

v0:
```python
import jax
import jax.numpy as jnp
from jax import lax
from jax.sharding import PartitionSpec as P

epsilon = 1e-05


def normalize(values, gain_vec, bias_vec):
    values = values.astype(jnp.float32)
    centred = values - jnp.mean(values, axis=-1, keepdims=True)
    inverse = lax.rsqrt(jnp.mean(centred * centred, axis=-1, keepdims=True) + epsilon)
    normed = centred * inverse
    return (normed * gain_vec + bias_vec, normed, inverse)


def norm_back(upstream, normed, inverse, gain_vec):
    scaled = upstream * gain_vec
    return inverse * (
        scaled
        - jnp.mean(scaled, axis=-1, keepdims=True)
        - normed * jnp.mean(scaled * normed, axis=-1, keepdims=True)
    )


def project(values, matrix):
    flat = values.reshape(-1, values.shape[-1])
    result = jnp.dot(flat, matrix, preferred_element_type=jnp.float32)
    return result.reshape(values.shape[:-1] + (matrix.shape[1],))


def weight_grad(left, right):
    return jnp.dot(
        left.reshape(-1, left.shape[-1]).T,
        right.reshape(-1, right.shape[-1]),
        preferred_element_type=jnp.float32,
    )


def channel_sum(values):
    return jnp.sum(values, axis=(0, 1))


def front(
    pair_map,
    saved_product,
    cotangent,
    pair_mask,
    ln_gain,
    ln_bias,
    out_gain,
    out_bias,
    w_a,
    w_ag,
    w_b,
    w_bg,
    w_g,
    w_o,
):
    pair_full, pair_hat, pair_inv = normalize(pair_map, ln_gain, ln_bias)
    normed_pair = pair_full.astype(jnp.bfloat16)
    proj_a = project(normed_pair, w_a)
    sig_a = jax.nn.sigmoid(project(normed_pair, w_ag))
    proj_b = project(normed_pair, w_b)
    sig_b = jax.nn.sigmoid(project(normed_pair, w_bg))
    gate_value = jax.nn.sigmoid(project(normed_pair, w_g))
    factor_a = (pair_mask * sig_a * proj_a).astype(jnp.bfloat16)
    factor_b = (pair_mask * sig_b * proj_b).astype(jnp.bfloat16)
    out_full, out_hat, out_inv = normalize(saved_product, out_gain, out_bias)
    normed_out = out_full.astype(jnp.bfloat16)
    update = project(normed_out, w_o)
    upstream = cotangent.astype(jnp.float32)
    grad_update = (upstream * gate_value).astype(jnp.bfloat16)
    grad_gate = (upstream * update * gate_value * (1.0 - gate_value)).astype(jnp.bfloat16)
    grad_normed_out = project(grad_update, w_o.T)
    grad_saved = norm_back(grad_normed_out, out_hat, out_inv, out_gain).astype(jnp.bfloat16)
    early = (
        weight_grad(normed_pair, grad_gate),
        weight_grad(normed_out, grad_update),
        channel_sum(grad_normed_out * out_hat),
        channel_sum(grad_normed_out),
    )
    kept = (normed_pair, pair_hat, pair_inv, proj_a, sig_a, proj_b, sig_b, grad_gate)
    return (factor_a, factor_b, grad_saved, early, kept)


def back(grad_fa, grad_fb, pair_mask, kept, ln_gain, w_a, w_ag, w_b, w_bg, w_g):
    normed_pair, pair_hat, pair_inv, proj_a, sig_a, proj_b, sig_b, grad_gate = kept
    masked_a = grad_fa * pair_mask
    masked_b = grad_fb * pair_mask
    grad_pa = (masked_a * sig_a).astype(jnp.bfloat16)
    grad_pag = (masked_a * proj_a * sig_a * (1.0 - sig_a)).astype(jnp.bfloat16)
    grad_pb = (masked_b * sig_b).astype(jnp.bfloat16)
    grad_pbg = (masked_b * proj_b * sig_b * (1.0 - sig_b)).astype(jnp.bfloat16)
    grad_zn = (
        project(grad_pa, w_a.T)
        + project(grad_pag, w_ag.T)
        + project(grad_pb, w_b.T)
        + project(grad_pbg, w_bg.T)
        + project(grad_gate, w_g.T)
    )
    grad_pair = norm_back(grad_zn, pair_hat, pair_inv, ln_gain).astype(jnp.bfloat16)
    late = (
        weight_grad(normed_pair, grad_pa),
        weight_grad(normed_pair, grad_pag),
        weight_grad(normed_pair, grad_pb),
        weight_grad(normed_pair, grad_pbg),
        channel_sum(grad_zn * pair_hat),
        channel_sum(grad_zn),
    )
    return (grad_pair, late)


def body(
    pair_map,
    saved_product,
    cotangent,
    residue_mask,
    ln_gain,
    ln_bias,
    out_gain,
    out_bias,
    w_a,
    w_ag,
    w_b,
    w_bg,
    w_g,
    w_o,
):
    row_count, col_count, channels = pair_map.shape
    row_first = lax.axis_index("row") * row_count
    col_first = lax.axis_index("col") * col_count
    row_mask = lax.dynamic_slice_in_dim(residue_mask, row_first, row_count, 0).astype(jnp.float32)
    col_mask = lax.dynamic_slice_in_dim(residue_mask, col_first, col_count, 0).astype(jnp.float32)
    pair_mask = (row_mask[:, None] * col_mask[None, :])[:, :, None]
    factor_a, factor_b, grad_saved, early, kept = front(
        pair_map,
        saved_product,
        cotangent,
        pair_mask,
        ln_gain,
        ln_bias,
        out_gain,
        out_bias,
        w_a,
        w_ag,
        w_b,
        w_bg,
        w_g,
        w_o,
    )
    grad_wg, grad_wo, grad_og, grad_ob = early
    upstream_all = lax.all_gather(grad_saved, "col", axis=1, tiled=True)
    window = upstream_all
    grad_fa = jnp.einsum(
        "ijc,jkc->ikc",
        window,
        lax.all_gather(factor_b, "row", axis=0, tiled=True),
        preferred_element_type=jnp.float32,
    )
    window = upstream_all
    grad_fb = lax.psum_scatter(
        jnp.einsum("ijc,ikc->jkc", window, factor_a, preferred_element_type=jnp.float32).astype(
            jnp.bfloat16
        ),
        "row",
        scatter_dimension=0,
        tiled=True,
    ).astype(jnp.float32)
    grad_pair, late = back(grad_fa, grad_fb, pair_mask, kept, ln_gain, w_a, w_ag, w_b, w_bg, w_g)
    grad_wa, grad_wag, grad_wb, grad_wbg, grad_lg, grad_lb = late
    grad_wa, grad_wag, grad_wb, grad_wbg, grad_lg, grad_lb, grad_wg, grad_wo, grad_og, grad_ob = (
        lax.psum(
            (
                grad_wa,
                grad_wag,
                grad_wb,
                grad_wbg,
                grad_lg,
                grad_lb,
                grad_wg,
                grad_wo,
                grad_og,
                grad_ob,
            ),
            ("row", "col"),
        )
    )
    inv_total = 1.0 / (row_count * lax.axis_size("row"))
    return (
        grad_pair,
        grad_wa * inv_total,
        grad_wag * inv_total,
        grad_wb * inv_total,
        grad_wbg * inv_total,
        grad_wg * inv_total,
        grad_wo * inv_total,
        grad_lg * inv_total,
        grad_lb * inv_total,
        grad_og * inv_total,
        grad_ob * inv_total,
    )


def solution(mesh):
    return jax.shard_map(
        body,
        mesh=mesh,
        in_specs=(
            P("row", "col", None),
            P("row", "col", None),
            P("row", "col", None),
            P(),
            P(),
            P(),
            P(),
            P(),
            P(),
            P(),
            P(),
            P(),
            P(),
            P(),
        ),
        out_specs=(P("row", "col", None), P(), P(), P(), P(), P(), P(), P(), P(), P(), P()),
        check_vma=False,
    )
```

profile of v0, /device:TPU:1, one launch (start us, length us, event | category | flops | bytes accessed | tf_op | source)
XLA Modules:
  0.0 934.2 jit_solution(4547155388445766747)
XLA Ops:
  8.8 1.8 fusion.31
  15.3 2.3 fusion.27
  18.6 2.4 multiply_convert_fusion.2
  22.1 82.1 %all-gather.5.cloned.1.call-done = bf16[48,768,128]{2,1,0:T(8,128)(2,1)} async-done(((bf16[48,48,128]{2,1,0:T(8,128)(2,1)}), bf16[48,768,128]{2,1,0:T(8,128)(2,1)}) %all-gather.5.cloned.1.call-update) | async-done | bytes 9437200 | tf_op jit(solution)/shard_map/all_gather | solution.py:153
  104.2 12.9 %copy.32 = bf16[48,768,128]{1,0,2:T(8,128)(2,1)} copy(bf16[48,768,128]{2,1,0:T(8,128)(2,1)} %all-gather.5.cloned.1.call-done) | data formatting | bytes 18874368 | tf_op jit(solution)/shard_map/all_gather | solution.py:153
  117.1 10.0 %fusion.72 = bf16[128,48,768]{2,1,0:T(8,128)(2,1)} fusion(bf16[48,48,128]{0,1,2:T(8,128)(2,1)S(1)} %copy.34, bf16[48,768,128]{1,0,2:T(8,128)(2,1)} %copy.32), kind=kOutput, calls=%fused_computation.109 | convolution fusion | flops 452984832 | bytes 19464192 | tf_op jit(solution)/shard_map/ijc,ikc->jkc/dot_general | solution.py:163
  127.1 14.0 %copy.36 = bf16[128,48,768]{0,1,2:T(8,128)(2,1)} copy(bf16[128,48,768]{2,1,0:T(8,128)(2,1)} %fusion.72) | data formatting | bytes 18874368 | tf_op jit(solution)/shard_map/ijc,ikc->jkc/dot_general | solution.py:163
  142.7 199.9 %reduce-scatter.2.cloned.1.call-done = bf16[48,48,128]{2,1,0:T(8,128)(2,1)} async-done(((bf16[768,48,128]{2,1,0:T(8,128)(2,1)}), bf16[48,48,128]{2,1,0:T(8,128)(2,1)}) %reduce-scatter.2.cloned.1.call-update) | async-done | bytes 589840 | tf_op jit(solution)/shard_map/reduce_scatter | solution.py:162
  342.6 3.7 multiply_convert_fusion
  346.6 2.2 fusion.23
  348.8 1.6 convolution_bitcast_fusion.1
  350.5 1.7 convolution_bitcast_fusion
  352.1 1.6 convolution_bitcast_fusion.2
  353.8 1.6 convolution_bitcast_fusion.3
  355.4 195.5 %all-gather.3.cloned.1.call-done = bf16[768,48,128]{2,1,0:T(8,128)(2,1)} async-done(((bf16[48,48,128]{2,1,0:T(8,128)(2,1)}), bf16[768,48,128]{2,1,0:T(8,128)(2,1)}) %all-gather.3.cloned.1.call-update) | async-done | bytes 9437200 | tf_op jit(solution)/shard_map/all_gather | solution.py:158
  550.9 14.0 %copy.31 = bf16[768,48,128]{0,1,2:T(8,128)(2,1)} copy(bf16[768,48,128]{2,1,0:T(8,128)(2,1)} %all-gather.3.cloned.1.call-done) | data formatting | bytes 18874368 | tf_op jit(solution)/shard_map/all_gather | solution.py:158
  564.9 10.8 %fusion.71 = f32[128,48,48]{2,1,0:T(8,128)} fusion(bf16[768,48,128]{0,1,2:T(8,128)(2,1)} %copy.31, bf16[48,768,128]{1,0,2:T(8,128)(2,1)} %copy.32), kind=kOutput, calls=%fused_computation.108 | convolution fusion | flops 452984832 | bytes 20054016 | tf_op jit(solution)/shard_map/ijc,jkc->ikc/dot_general | solution.py:155
  575.7 3.4 copy.33
  579.1 1.6 multiply_convert_fusion.3
  580.8 1.7 convolution_bitcast_fusion.5
  582.8 1.7 convolution_bitcast_fusion.4
  589.4 78.1 %all-reduce = (f32[128]{0:T(128)S(1)}, f32[128]{0:T(128)S(1)}, f32[128]{0:T(128)S(1)}, f32[128]{0:T(128)S(1)}) all-reduce(f32[128]{0:T(128)S(1)} %get-tuple-element.13, f32[128]{0:T(128)S(1)} %get-tuple-element.18, f32[128]{0:T(128)S(1)} %get-tuple-element.11, ...), channel_id=1, replica_groups=mesh['row'=16,'col'=16] {'row','col'}, use_global_device_ids=true, to_apply=%region_16.0 | all-reduce | flops 512 | bytes 4096 | tf_op jit(solution)/shard_map/psum | solution.py:173
  669.0 2.3 fusion.37
  671.9 246.9 %all-reduce.4.cloned.1.call-done = (f32[128,128]{1,0:T(8,128)}, f32[128,128]{1,0:T(8,128)}, f32[128,128]{1,0:T(8,128)}, f32[128,128]{1,0:T(8,128)}, f32[128,128]{1,0:T(8,128)}, /*index=5*/f32[128,128]{1,0:T(8,128)}) async-done(((f32[128,128]{1,0:T(8,128)}, f32[128,128]{1,0:T(8,128)}, f32[128,128]{1,0:T(8,128)}, f32[128,128]{1,0:T(8,128)}, f32[128,128]{1,0:T(8,128)}, /*index=5*/f32[128,128]{1,0:T(8,128)}), ...) | async-done | bytes 393232 | tf_op jit(solution)/shard_map/psum | solution.py:173
  (104 shorter events, 26.1 us)
Async XLA Ops:
  7.2 335.4 %copy-start = (bf16[128,128]{1,0:T(8,128)(2,1)S(1)}, bf16[128,128]{1,0:T(8,128)(2,1)}, u32[]{:S(2)}) copy-start(bf16[128,128]{1,0:T(8,128)(2,1)} %param.25) | copy-start | bytes 98308
  7.2 3.4 copy-start.1
  7.2 97.0 %all-gather.5.cloned.1.call-start = ((), (), s32[]{:S(2)}) async-start(), calls=%async_computation.2 | async-start | bytes 10027008 | tf_op jit(solution)/shard_map/all_gather | solution.py:153
  8.8 3.9 copy-start.17
  8.8 3.9 copy-start.18
  8.8 3.9 copy-start.25
  10.6 4.7 copy-start.13
  15.3 2.4 copy-start.15
  17.7 324.9 %reduce-scatter.2.cloned.1.call-start = ((), (), s32[]{:S(2)}) async-start(), calls=%async_computation.3 | async-start | bytes 10027008 | tf_op jit(solution)/shard_map/reduce_scatter | solution.py:162
  18.6 2.5 copy-start.3
  141.1 409.8 %all-gather.3.cloned.1.call-start = ((), (), s32[]{:S(2)}) async-start(), calls=%async_computation.1 | async-start | bytes 10027008 | tf_op jit(solution)/shard_map/all_gather | solution.py:158
  142.6 203.9 %copy-start.14 = (f32[48,48]{1,0:T(8,128)S(1)}, f32[48,48]{1,0:T(8,128)}, u32[]{:S(2)}) copy-start(f32[48,48]{1,0:T(8,128)} %copy-done.13) | copy-start | bytes 27652
  142.6 203.9 %copy-start.20 = (f32[128]{0:T(128)S(1)}, f32[128]{0:T(128)}, u32[]{:S(2)}) copy-start(f32[128]{0:T(128)} %param.20) | copy-start | bytes 1540
  142.7 203.9 %copy-start.24 = (bf16[128,128]{1,0:T(8,128)(2,1)S(1)}, bf16[128,128]{1,0:T(8,128)(2,1)}, u32[]{:S(2)}) copy-start(bf16[128,128]{1,0:T(8,128)(2,1)} %param.27) | copy-start | bytes 98308
  142.7 203.9 %copy-start.27 = (f32[128]{0:T(128)S(1)}, f32[128]{0:T(128)}, u32[]{:S(2)}) copy-start(f32[128]{0:T(128)} %param.21) | copy-start | bytes 1540
  346.3 5.8 copy-start.7
  346.3 572.5 %all-reduce.4.cloned.1.call-start = ((), (), s32[]{:S(2)}) async-start(), calls=%async_computation.4 | async-start | bytes 786432 | tf_op jit(solution)/shard_map/psum | solution.py:173
  348.8 1.7 copy-start.30
  348.8 1.7 copy-start.22
  348.8 1.7 copy-start.29
  575.7 3.4 copy-start.4
  575.7 3.4 copy-start.5
  580.8 2.0 copy-start.6
  582.8 1.7 copy-start.16
  (12 other events, 13.6 us)
Sparse Core Ops, SparseCore 0:
  17.8 86.3 all-gather.4
  141.2 201.2 reduce-scatter.1
  346.4 204.3 all-gather.2
  671.5 247.2 all-reduce.3
where the time goes:
time: 936 us; the launch traced here: 934 us
  waiting for transfers between devices  724 us (77%)
  blocking collectives  78.1 us (8%)
  local copies, waits for them, and re-layouts  48.1 us (5%)
  matrix products  46.5 us (5%)
  other arithmetic  22.5 us (2%)
  between operations  14.2 us (2%)
    psum x1, waiting for transfers between devices, body(): lax.psum((grad_wa, grad_wag, grad_wb, grad_wbg, grad_lg, grad_lb, grad_wg...  247 us
    reduce_scatter x1, waiting for transfers between devices, body(): lax.psum_scatter(jnp.einsum('ijc,ikc->jkc', window, factor_a, preferred_e...  200 us
    all_gather x1, waiting for transfers between devices, body(): lax.all_gather(factor_b, 'row', axis=0, tiled=True)  195 us
    all_gather x1, waiting for transfers between devices, body(): upstream_all = lax.all_gather(grad_saved, 'col', axis=1, tiled=True)  82.1 us
    psum x1, blocking collectives, body(): lax.psum((grad_wa, grad_wag, grad_wb, grad_wbg, grad_lg, grad_lb, grad_wg...  78.1 us
  transfers between devices with their start and end apart: 4, of which 4 were waited for; matrix products, arithmetic and copies ran while one was open for 2% of the time, Pallas kernels for 0%

commit v1 on v0

v1 whole, which is shorter than its diff:
```python
import jax
import jax.numpy as jnp
from jax import lax
from jax.experimental import pallas as pl
from jax.experimental.pallas import tpu as pltpu
from jax.sharding import PartitionSpec as P

MESH = pl.DeviceIdType.MESH
f32 = jnp.float32
bf16 = jnp.bfloat16
epsilon = 1e-05
VMEM = pl.BlockSpec(memory_space=pltpu.VMEM)
LIMIT = 56 << 20

DEV = 16
BLK = 48
CH = 128
PACK = 8
GROUPS = BLK // PACK
LANES = PACK * BLK
TILES = LANES // 128
CPD = CH // DEV
ROWS = GROUPS * CPD
CROWS = GROUPS * DEV
N = DEV * BLK
STEP = 16
CELLS = STEP * BLK
NSTEP = BLK // STEP
SUMROWS = 64


def dot(a, b, ca=1, cb=0):
    return lax.dot_general(a, b, (((ca,), (cb,)), ((), ())), preferred_element_type=f32)


def mean(v):
    return jnp.mean(v, axis=-1, keepdims=True)


def normalize(values):
    values = values.astype(f32)
    centred = values - mean(values)
    inverse = lax.rsqrt(mean(centred * centred) + epsilon)
    return centred * inverse, inverse


def norm_back(scaled, normed, inverse):
    return inverse * (scaled - mean(scaled) - normed * mean(scaled * normed))


def to_channels(ref, values):
    halves = []
    for g in range(STEP // PACK):
        turned = values[g * LANES : (g + 1) * LANES].T
        halves.append(turned.reshape(DEV, CPD, LANES))
    ref[...] = jnp.concatenate(halves, axis=1).astype(bf16)


def from_channels(ref):
    values = ref[...].astype(f32)
    parts = []
    for g in range(STEP // PACK):
        parts.append(values[:, g * CPD : (g + 1) * CPD, :].reshape(CH, LANES).T)
    return jnp.concatenate(parts, axis=0)


def front_kernel(
    pm, sp, ct, rm, km, vec, wcat, wo, gx_t, fa_t, fb_t, a1, a2, b1, b2, gg, gwo, gvec
):
    step = pl.program_id(0)
    mask = jnp.broadcast_to(rm[...][:, None, :] * km[...][None], (STEP, BLK, CH)).reshape(CELLS, CH)
    ln_gain, ln_bias, out_gain, out_bias = (vec[i : i + 1, :] for i in range(4))
    hat, _ = normalize(pm[...].reshape(CELLS, CH))
    zn = (hat * ln_gain + ln_bias).astype(bf16)
    pa, pag, pb, pbg, pg = (dot(zn, wcat[:, i * CH : (i + 1) * CH]) for i in range(5))
    sig_a = jax.nn.sigmoid(pag)
    ma = mask * sig_a
    fa = ma * pa
    a1[...] = ma
    a2[...] = fa * (1.0 - sig_a)
    to_channels(fa_t, fa)
    sig_b = jax.nn.sigmoid(pbg)
    mb = mask * sig_b
    fb = mb * pb
    b1[...] = mb
    b2[...] = fb * (1.0 - sig_b)
    to_channels(fb_t, fb)
    gate = jax.nn.sigmoid(pg)
    ohat, oinv = normalize(sp[...].reshape(CELLS, CH))
    xn = (ohat * out_gain + out_bias).astype(bf16)
    update = dot(xn, wo[...])
    up = ct[...].reshape(CELLS, CH).astype(f32) * gate
    gu = up.astype(bf16)
    gg[...] = (up * update * (1.0 - gate)).astype(bf16)
    gxn = dot(gu, wo[...], 1, 1)
    to_channels(gx_t, norm_back(gxn * out_gain, ohat, oinv))
    gw = dot(xn, gu, 0, 0)
    sums = jnp.concatenate(
        [
            jnp.sum(gxn * ohat, axis=0, keepdims=True),
            jnp.sum(gxn, axis=0, keepdims=True),
            jnp.zeros((6, CH), f32),
        ],
        axis=0,
    )

    @pl.when(step == 0)
    def _():
        gwo[...] = gw
        gvec[...] = sums

    @pl.when(step > 0)
    def _():
        gwo[...] += gw
        gvec[...] += sums


def whole(*shape):
    return pl.BlockSpec(shape, lambda i: (0,) * len(shape))


def front(pm, sp, ct, rm, km, vec, wcat, wo):
    cells = pl.BlockSpec((STEP, BLK, CH), lambda i: (i, 0, 0))
    flat = pl.BlockSpec((CELLS, CH), lambda i: (i, 0))
    turned = pl.BlockSpec((DEV, STEP // PACK * CPD, LANES), lambda i: (0, i, 0))
    t_shape = jax.ShapeDtypeStruct((DEV, ROWS, LANES), bf16)
    c_shape = jax.ShapeDtypeStruct((BLK * BLK, CH), f32)
    return pl.pallas_call(
        front_kernel,
        grid=(NSTEP,),
        in_specs=[
            cells,
            cells,
            cells,
            pl.BlockSpec((STEP, CH), lambda i: (i, 0)),
            whole(BLK, CH),
            whole(8, CH),
            whole(CH, 5 * CH),
            whole(CH, CH),
        ],
        out_specs=[turned] * 3 + [flat] * 5 + [whole(CH, CH), whole(8, CH)],
        out_shape=[t_shape] * 3
        + [c_shape] * 4
        + [
            jax.ShapeDtypeStruct((BLK * BLK, CH), bf16),
            jax.ShapeDtypeStruct((CH, CH), f32),
            jax.ShapeDtypeStruct((8, CH), f32),
        ],
        name="front",
        compiler_params=pltpu.CompilerParams(vmem_limit_bytes=LIMIT),
    )(pm, sp, ct, rm, km, vec, wcat, wo)


def back_kernel(pm, gfa, gfb, a1, a2, b1, b2, gg, vec, wcat, gp, gw, gvec):
    step = pl.program_id(0)
    ln_gain, ln_bias = vec[0:1, :], vec[1:2, :]
    hat, inv = normalize(pm[...].reshape(CELLS, CH))
    zn = (hat * ln_gain + ln_bias).astype(bf16)
    ga = from_channels(gfa)
    gb = from_channels(gfb)
    grads = jnp.concatenate(
        [
            (ga * a1[...]).astype(bf16),
            (ga * a2[...]).astype(bf16),
            (gb * b1[...]).astype(bf16),
            (gb * b2[...]).astype(bf16),
            gg[...],
        ],
        axis=1,
    )
    gz = dot(grads, wcat[...], 1, 1)
    gp[...] = norm_back(gz * ln_gain, hat, inv).astype(bf16).reshape(STEP, BLK, CH)
    part = dot(zn, grads, 0, 0)
    sums = jnp.concatenate(
        [
            jnp.sum(gz * hat, axis=0, keepdims=True),
            jnp.sum(gz, axis=0, keepdims=True),
            jnp.zeros((6, CH), f32),
        ],
        axis=0,
    )

    @pl.when(step == 0)
    def _():
        gw[...] = part
        gvec[...] = sums

    @pl.when(step > 0)
    def _():
        gw[...] += part
        gvec[...] += sums


def back(pm, gfa, gfb, a1, a2, b1, b2, gg, vec, wcat):
    cells = pl.BlockSpec((STEP, BLK, CH), lambda i: (i, 0, 0))
    flat = pl.BlockSpec((CELLS, CH), lambda i: (i, 0))
    turned = pl.BlockSpec((DEV, STEP // PACK * CPD, LANES), lambda i: (0, i, 0))
    return pl.pallas_call(
        back_kernel,
        grid=(NSTEP,),
        in_specs=[cells, turned, turned] + [flat] * 5 + [whole(8, CH), whole(CH, 5 * CH)],
        out_specs=[cells, whole(CH, 5 * CH), whole(8, CH)],
        out_shape=[
            jax.ShapeDtypeStruct((BLK, BLK, CH), bf16),
            jax.ShapeDtypeStruct((CH, 5 * CH), f32),
            jax.ShapeDtypeStruct((8, CH), f32),
        ],
        name="back",
        compiler_params=pltpu.CompilerParams(vmem_limit_bytes=LIMIT),
    )(pm, gfa, gfb, a1, a2, b1, b2, gg, vec, wcat)


def peer(axis, d):
    return lax.rem(lax.axis_index(axis) + d, DEV)


def greet(axes):
    barrier = pltpu.get_barrier_semaphore()
    for axis in axes:

        def hello(d, carry):
            pl.semaphore_signal(
                barrier, inc=1, device_id={axis: peer(axis, d)}, device_id_type=MESH
            )
            return carry

        lax.fori_loop(1, DEV, hello, 0)
    pl.semaphore_wait(barrier, len(axes) * (DEV - 1))


def each(action):
    def run(d, carry):
        action(d)
        return carry

    lax.fori_loop(1, DEV, run, 0)


def copier(axis, src, dst, send, recv):
    def make(d):
        t = peer(axis, d)
        return pltpu.make_async_remote_copy(
            src_ref=src(t),
            dst_ref=dst,
            send_sem=send.at[d],
            recv_sem=recv.at[d],
            device_id={axis: t},
            device_id_type=MESH,
        )

    return make


def there_kernel(
    gx, fa, fb, gout, fout, rbuf, scr, sbuf, r_send, r_recv, c_send, c_recv, r_loc, c_loc
):
    row, col = lax.axis_index("row"), lax.axis_index("col")
    arrays = (gx, fa, fb)
    own = [
        pltpu.make_async_copy(arrays[a].at[row], rbuf.at[a, row], r_loc.at[a]) for a in range(3)
    ]
    for o in own:
        o.start()
    greet(("row", "col"))
    rows = [
        copier(
            "row",
            lambda t, a=a: arrays[a].at[t],
            rbuf.at[a, row],
            r_send.at[a],
            r_recv.at[a],
        )
        for a in range(3)
    ]
    for a in range(3):
        each(lambda d, a=a: rows[a](d).start())

    def shuffle(a):
        own[a].wait()
        each(lambda d: rows[a](d).wait_recv())
        for t in range(TILES):
            lanes = slice(t * 128, (t + 1) * 128)
            scr[t] = rbuf[a, :, :, lanes].reshape(DEV * ROWS, 128).astype(f32)
            for m in range(CPD):
                sbuf[a, m, :, lanes] = scr[t, pl.ds(m, CROWS, stride=CPD), :].astype(bf16)

    g_copy = copier("col", lambda t: sbuf.at[0, t // 2], gout.at[col], c_send.at[0], c_recv.at[0])
    f_copy = copier(
        "col",
        lambda t: sbuf.at[2 - lax.rem(t, 2), t // 2],
        fout.at[col],
        c_send.at[1],
        c_recv.at[1],
    )
    shuffle(0)
    own_g = pltpu.make_async_copy(sbuf.at[0, col // 2], gout.at[col], c_loc.at[0])
    own_g.start()
    each(lambda d: g_copy(d).start())
    shuffle(1)
    shuffle(2)
    own_f = pltpu.make_async_copy(sbuf.at[2 - lax.rem(col, 2), col // 2], fout.at[col], c_loc.at[1])
    own_f.start()
    each(lambda d: f_copy(d).start())
    for a in range(3):
        each(lambda d, a=a: rows[a](d).wait_send())
    own_g.wait()
    each(lambda d: g_copy(d).wait())
    own_f.wait()
    each(lambda d: f_copy(d).wait())


def there(gx, fa, fb):
    shape = jax.ShapeDtypeStruct((DEV, CROWS, LANES), bf16)
    dma = pltpu.SemaphoreType.DMA
    return pl.pallas_call(
        there_kernel,
        in_specs=[VMEM] * 3,
        out_specs=[VMEM] * 2,
        out_shape=[shape] * 2,
        scratch_shapes=[
            pltpu.VMEM((3, DEV, ROWS, LANES), bf16),
            pltpu.VMEM((TILES, DEV * ROWS, 128), f32),
            pltpu.VMEM((3, CPD, CROWS, LANES), bf16),
            dma((3, DEV)),
            dma((3, DEV)),
            dma((2, DEV)),
            dma((2, DEV)),
            dma((3,)),
            dma((2,)),
        ],
        name="there",
        compiler_params=pltpu.CompilerParams(
            collective_id=1, has_side_effects=True, vmem_limit_bytes=LIMIT
        ),
    )(gx, fa, fb)


def home_kernel(g, ga, gb, cbuf, scr, sbuf, c_send, c_recv, r_send, r_recv, loc):
    row, col = lax.axis_index("row"), lax.axis_index("col")
    outs = (ga, gb)
    own = pltpu.make_async_copy(g.at[col], cbuf.at[col], loc.at[0])
    own.start()
    greet(("row", "col"))
    cols = copier("col", lambda t: g.at[t], cbuf.at[col], c_send, c_recv)
    each(lambda d: cols(d).start())
    own.wait()
    each(lambda d: cols(d).wait_recv())
    rows = [
        copier(
            "row", lambda t, h=h: sbuf.at[h, t], outs[h].at[row], r_send.at[h], r_recv.at[h]
        )
        for h in range(2)
    ]
    mine = []
    for h in range(2):
        for t in range(TILES):
            lanes = slice(t * 128, (t + 1) * 128)
            for m in range(CPD):
                scr[t, pl.ds(m, CROWS, stride=CPD), :] = cbuf[2 * m + h, :, lanes].astype(f32)
            sbuf[h, :, :, lanes] = scr[t].reshape(DEV, ROWS, 128).astype(bf16)
        mine.append(pltpu.make_async_copy(sbuf.at[h, row], outs[h].at[row], loc.at[1 + h]))
        mine[h].start()
        each(lambda d, h=h: rows[h](d).start())
    each(lambda d: cols(d).wait_send())
    for h in range(2):
        mine[h].wait()
        each(lambda d, h=h: rows[h](d).wait())


def home(g):
    shape = jax.ShapeDtypeStruct((DEV, ROWS, LANES), bf16)
    dma = pltpu.SemaphoreType.DMA
    return pl.pallas_call(
        home_kernel,
        in_specs=[VMEM],
        out_specs=[VMEM] * 2,
        out_shape=[shape] * 2,
        scratch_shapes=[
            pltpu.VMEM((DEV, CROWS, LANES), bf16),
            pltpu.VMEM((TILES, DEV * ROWS, 128), f32),
            pltpu.VMEM((2, DEV, ROWS, LANES), bf16),
            dma((DEV,)),
            dma((DEV,)),
            dma((2, DEV)),
            dma((2, DEV)),
            dma((3,)),
        ],
        name="home",
        compiler_params=pltpu.CompilerParams(
            collective_id=2, has_side_effects=True, vmem_limit_bytes=LIMIT
        ),
    )(g)


NT = N // 128


def assemble(src, scr, dst):
    for a in range(PACK):
        rows = jnp.concatenate(
            [src[q][:, a * BLK : (a + 1) * BLK].astype(f32) for q in range(DEV)], axis=1
        )
        for t in range(NT):
            scr[t, pl.ds(a, CROWS, stride=PACK), :] = rows[:, t * 128 : (t + 1) * 128]
    for t in range(NT):
        dst[:, t * 128 : (t + 1) * 128] = scr[t].astype(bf16)


def product_kernel(g, f, out, scr, gfull, ffull):
    assemble(g, scr, gfull)
    assemble(f, scr, ffull)
    odd = lax.rem(lax.axis_index("col"), 2)

    def spread(values):
        for t in range(NT):
            scr[t] = values[:, t * 128 : (t + 1) * 128]

    @pl.when(odd == 0)
    def _():
        spread(dot(gfull[...], ffull[...]))

    @pl.when(odd == 1)
    def _():
        spread(dot(gfull[...], ffull[...], 0, 0))

    rows = [[scr[t, pl.ds(a, CROWS, stride=PACK), :] for t in range(NT)] for a in range(PACK)]

    def piece(a, q):
        lo, hi = q * BLK, (q + 1) * BLK
        first, last = lo // 128, (hi - 1) // 128
        if first == last:
            return rows[a][first][:, lo - first * 128 : hi - first * 128]
        return jnp.concatenate(
            [rows[a][first][:, lo - first * 128 :], rows[a][last][:, : hi - last * 128]], axis=1
        )

    for q in range(DEV):
        out[q] = jnp.concatenate([piece(a, q) for a in range(PACK)], axis=1).astype(bf16)


def product(g, f):
    return pl.pallas_call(
        product_kernel,
        in_specs=[VMEM] * 2,
        out_specs=VMEM,
        out_shape=jax.ShapeDtypeStruct((DEV, CROWS, LANES), bf16),
        scratch_shapes=[
            pltpu.VMEM((NT, N, 128), f32),
            pltpu.VMEM((N, N), bf16),
            pltpu.VMEM((N, N), bf16),
        ],
        name="product",
        compiler_params=pltpu.CompilerParams(vmem_limit_bytes=LIMIT),
    )(g, f)


def sum_kernel(gw, gwo, gvec, lvec, out, part, got1, mid, got2, fin, sem_s, sem_r, loc):
    row, col = lax.axis_index("row"), lax.axis_index("col")
    for k in range(5):
        for j in range(2):
            part[2 * k + j] = gw[j * 64 : (j + 1) * 64, k * CH : (k + 1) * CH].astype(bf16)
    for j in range(2):
        part[10 + j] = gwo[j * 64 : (j + 1) * 64, :].astype(bf16)
    part[12] = jnp.concatenate(
        [lvec[...], gvec[...], jnp.zeros((SUMROWS - 16, CH), f32)], axis=0
    ).astype(bf16)
    part[13:16] = jnp.zeros((3, SUMROWS, CH), bf16)
    own = pltpu.make_async_copy(part.at[col], got1.at[col], loc.at[0])
    own.start()
    greet(("row", "col"))
    one = copier("col", lambda t: part.at[t], got1.at[col], sem_s.at[0], sem_r.at[0])
    each(lambda d: one(d).start())
    own.wait()
    each(lambda d: one(d).wait())
    mid[...] = jnp.sum(got1[...].astype(f32), axis=0).astype(bf16)
    own = pltpu.make_async_copy(mid, got2.at[row], loc.at[1])
    own.start()
    two = copier("row", lambda t: mid, got2.at[row], sem_s.at[1], sem_r.at[1])
    each(lambda d: two(d).start())
    own.wait()
    each(lambda d: two(d).wait())
    fin[...] = (jnp.sum(got2[...].astype(f32), axis=0) * (1.0 / N)).astype(bf16)
    own = pltpu.make_async_copy(fin, out.at[col], loc.at[2])
    own.start()
    three = copier("col", lambda t: fin, out.at[col], sem_s.at[2], sem_r.at[2])
    each(lambda d: three(d).start())
    own.wait()
    each(lambda d: three(d).wait())


def sum_all(gw, gwo, gvec, lvec):
    dma = pltpu.SemaphoreType.DMA
    wide = (DEV, SUMROWS, CH)
    return pl.pallas_call(
        sum_kernel,
        in_specs=[VMEM] * 4,
        out_specs=VMEM,
        out_shape=jax.ShapeDtypeStruct(wide, bf16),
        scratch_shapes=[
            pltpu.VMEM(wide, bf16),
            pltpu.VMEM(wide, bf16),
            pltpu.VMEM((SUMROWS, CH), bf16),
            pltpu.VMEM(wide, bf16),
            pltpu.VMEM((SUMROWS, CH), bf16),
            dma((3, DEV)),
            dma((3, DEV)),
            dma((3,)),
        ],
        name="sum_all",
        compiler_params=pltpu.CompilerParams(
            collective_id=3, has_side_effects=True, vmem_limit_bytes=LIMIT
        ),
    )(gw, gwo, gvec, lvec)


def finish_kernel(s, *outs):
    for k in range(6):
        for j in range(2):
            outs[k][j * 64 : (j + 1) * 64, :] = s[2 * k + j].astype(f32)
    vec = s[12].astype(f32)
    outs[6][...] = vec[0:1]
    outs[7][...] = vec[1:2]
    outs[8][...] = vec[8:9]
    outs[9][...] = vec[9:10]


def finish(s):
    return pl.pallas_call(
        finish_kernel,
        in_specs=[VMEM],
        out_specs=[VMEM] * 10,
        out_shape=[jax.ShapeDtypeStruct((CH, CH), f32)] * 6
        + [jax.ShapeDtypeStruct((1, CH), f32)] * 4,
        name="finish",
    )(s)


def body(
    pair_map,
    saved_product,
    cotangent,
    residue_mask,
    ln_gain,
    ln_bias,
    out_gain,
    out_bias,
    w_a,
    w_ag,
    w_b,
    w_bg,
    w_g,
    w_o,
):
    row_first = lax.axis_index("row") * BLK
    col_first = lax.axis_index("col") * BLK
    row_mask = lax.dynamic_slice_in_dim(residue_mask, row_first, BLK, 0).astype(f32)
    col_mask = lax.dynamic_slice_in_dim(residue_mask, col_first, BLK, 0).astype(f32)
    rm = jnp.broadcast_to(row_mask[:, None], (BLK, CH))
    km = jnp.broadcast_to(col_mask[:, None], (BLK, CH))
    vec = jnp.concatenate(
        [jnp.stack([ln_gain, ln_bias, out_gain, out_bias]), jnp.zeros((4, CH), f32)], axis=0
    )
    wcat = jnp.concatenate([w_a, w_ag, w_b, w_bg, w_g], axis=1)
    gx, fa, fb, a1, a2, b1, b2, gg, gwo, gvec = front(
        pair_map, saved_product, cotangent, rm, km, vec, wcat, w_o
    )
    gall, fall = there(gx, fa, fb)
    gfa, gfb = home(product(gall, fall))
    grad_pair, gw, lvec = back(pair_map, gfa, gfb, a1, a2, b1, b2, gg, vec, wcat)
    outs = finish(sum_all(gw, gwo, gvec, lvec))
    return (grad_pair,) + tuple(outs[:6]) + tuple(v.reshape(CH) for v in outs[6:])


def solution(mesh):
    return jax.shard_map(
        body,
        mesh=mesh,
        in_specs=(P("row", "col", None),) * 3 + (P(),) * 11,
        out_specs=(P("row", "col", None),) + (P(),) * 10,
        check_vma=False,
    )
```

time: 936 us -> 190 us (0.20)
  waiting for transfers between devices: 724 us -> 0 us
  Pallas kernels: 0 us -> 181 us
  blocking collectives: 78.1 us -> 0 us
  matrix products: 46.5 us -> 0 us
  local copies, waits for them, and re-layouts: 48.1 us -> 7.18 us
  other arithmetic: 22.5 us -> 0.84 us
  between operations: 14.2 us -> 0.82 us
    all_gather x2 -> x0, waiting for transfers between devices: 278 us -> none  [the longest x1 195 us: body(): lax.all_gather(factor_b, 'row', axis=0, tiled=True)]
    psum x1 -> x0, waiting for transfers between devices: 247 us -> none  [body(): lax.psum((grad_wa, grad_wag, grad_wb, grad_wbg, grad_lg, grad_lb, grad_wg...]
    reduce_scatter x1 -> x0, waiting for transfers between devices: 200 us -> none  [body(): lax.psum_scatter(jnp.einsum('ijc,ikc->jkc', window, factor_a, preferred_e...]
    pallas_call x0 -> x7, Pallas kernels: none -> 181 us  [the longest x1 72.1 us: there(): pl.pallas_call(there_kernel, in_specs=[VMEM] * 3, out_specs=[VMEM] * 2, o...]
    psum x1 -> x0, blocking collectives: 78.1 us -> none  [body(): lax.psum((grad_wa, grad_wag, grad_wb, grad_wbg, grad_lg, grad_lb, grad_wg...]
    dot_general x20 -> x0, matrix products: 46.5 us -> none  [the longest x12 15.8 us: project(): result = jnp.dot(flat, matrix, preferred_element_type=jnp.float32)]
    all_gather x2 -> x0, local copies, waits for them, and re-layouts: 26.9 us -> none  [the longest x1 14 us: body(): lax.all_gather(factor_b, 'row', axis=0, tiled=True)]
    dot_general x2 -> x0, local copies, waits for them, and re-layouts: 17.4 us -> none  [the longest x1 14 us: body(): jnp.einsum('ijc,ikc->jkc', window, factor_a, preferred_element_type=jnp.f...]
  transfers between devices with their start and end apart: 4 -> 0, of which waited for: 4 -> 0; matrix products, arithmetic and copies ran while one was open for 2% -> 0% of each run, Pallas kernels for 0% -> 0%
where the time goes in v1:
time: 190 us; the launch traced here: 189 us
  Pallas kernels  181 us (95%)
  local copies, waits for them, and re-layouts  7.18 us (4%)
    pallas_call x1, Pallas kernels, there(): pl.pallas_call(there_kernel, in_specs=[VMEM] * 3, out_specs=[VMEM] * 2, o...  72.1 us
    pallas_call x1, Pallas kernels, home(): pl.pallas_call(home_kernel, in_specs=[VMEM], out_specs=[VMEM] * 2, out_sh...  54 us
    pallas_call x1, Pallas kernels, sum_all(): pl.pallas_call(sum_kernel, in_specs=[VMEM] * 4, out_specs=VMEM, out_shape...  29.9 us
    pallas_call x1, Pallas kernels, product(): pl.pallas_call(product_kernel, in_specs=[VMEM] * 2, out_specs=VMEM, out_s...  9.17 us
    pallas_call x1, Pallas kernels, front(): pl.pallas_call(front_kernel, grid=(NSTEP,), in_specs=[cells, cells, cells...  7.23 us
    pallas_call x1, Pallas kernels, back(): pl.pallas_call(back_kernel, grid=(NSTEP,), in_specs=[cells, turned, turne...  6.47 us

profile of v1, /device:TPU:1, one launch (start us, length us, event | category | flops | bytes accessed | tf_op | source)
XLA Modules:
  0.0 189.4 jit_solution(15503821340034409889)
XLA Ops:
  0.6 0.8 dynamic-slice_convert_fusion
  1.5 1.3 concatenate.6.vec
  2.8 0.7 broadcast_in_dim.7.km
  3.5 0.7 broadcast_in_dim.6.rm
  4.2 0.8 constant_dynamic-update-slice_fusion.4
  4.9 0.8 constant_dynamic-update-slice_fusion.3
  5.7 0.8 constant_dynamic-update-slice_fusion.2
  6.5 0.8 constant_dynamic-update-slice_fusion.1
  7.2 0.8 constant_dynamic-update-slice_fusion.wcat
  8.0 0.0 copy-start
  8.0 0.7 copy-done
  8.7 7.2 %front.1 = (bf16[16,48,384]{2,1,0:T(8,128)(2,1)}, bf16[16,48,384]{2,1,0:T(8,128)(2,1)}, bf16[16,48,384]{2,1,0:T(8,128)(2,1)}, f32[2304,128]{1,0:T(8,128)}, f32[2...) custom-call(bf16[48,48,128]{2,1,0:T(8,128)(2,1)} %pm.3, ...), custom_call_target="tpu_custom_call" | custom-call | tf_op jit(solution)/shard_map/front/pallas_call | solution.py:128
  15.9 72.1 %there.1 = (bf16[16,96,384]{2,1,0:T(8,128)(2,1)}, bf16[16,96,384]{2,1,0:T(8,128)(2,1)}) custom-call(bf16[16,48,384]{2,1,0:T(8,128)(2,1)} %get-tuple-element.38.gx, bf16[16,48,384]{2,1,0:T(8,128)(2,1)} %get-tuple-element.39.fa, bf16[16,48,384]{2,1,0:T(8,128)(2,1)} %get-tuple-element.40.fb), custom_call_target="tpu_custom_call" | custom-call | tf_op jit(solution)/shard_map/there/pallas_call | solution.py:315
  88.0 9.2 %product.1.g = bf16[16,96,384]{2,1,0:T(8,128)(2,1)} custom-call(bf16[16,96,384]{2,1,0:T(8,128)(2,1)} %get-tuple-element.41.g, bf16[16,96,384]{2,1,0:T(8,128)(2,1)} %get-tuple-element.42.f), custom_call_target="tpu_custom_call" | custom-call | tf_op jit(solution)/shard_map/product/pallas_call | solution.py:442
  97.2 54.0 %home.1 = (bf16[16,48,384]{2,1,0:T(8,128)(2,1)}, bf16[16,48,384]{2,1,0:T(8,128)(2,1)}) custom-call(bf16[16,96,384]{2,1,0:T(8,128)(2,1)} %product.1.g), custom_call_target="tpu_custom_call" | custom-call | tf_op jit(solution)/shard_map/home/pallas_call | solution.py:373
  151.2 6.5 %back.1 = (bf16[48,48,128]{2,1,0:T(8,128)(2,1)}, f32[128,640]{1,0:T(8,128)}, f32[8,128]{1,0:T(8,128)}) custom-call(bf16[48,48,128]{2,1,0:T(8,128)(2,1)} %pm.3, bf16[16,48,384]{2,1,0:T(8,128)(2,1)} %get-tuple-element.43.gfa, bf16[16,48,384]{2,1,0:T(8,128)(2,1)} %get-tuple-element.44.gfb, f32[2304,128]{1,0:T(8,128)} %get-tuple-element.45.a1, ...), custom_call_target="tpu_custom_call" | custom-call | tf_op jit(solution)/shard_map/back/pallas_call | solution.py:198
  157.7 29.9 %sum_all.1.s = bf16[16,64,128]{2,1,0:T(8,128)(2,1)} custom-call(f32[128,640]{1,0:T(8,128)} %get-tuple-element.51.gw, f32[128,128]{1,0:T(8,128)} %get-tuple-element.52.gwo, f32[8,128]{1,0:T(8,128)} %get-tuple-element.53.gvec, f32[8,128]{1,0:T(8,128)} %get-tuple-element.54.lvec), custom_call_target="tpu_custom_call" | custom-call | tf_op jit(solution)/shard_map/sum_all/pallas_call | solution.py:494
  187.6 1.7 finish.1
  (1 shorter events, 0.0 us)
Async XLA Ops:
  8.0 0.7 copy-start

commit v2 on v1

v2 whole, which is shorter than its diff:
```python
import jax
import jax.numpy as jnp
from jax import lax
from jax.experimental import pallas as pl
from jax.experimental.pallas import tpu as pltpu
from jax.sharding import PartitionSpec as P

MESH = pl.DeviceIdType.MESH
f32 = jnp.float32
bf16 = jnp.bfloat16
epsilon = 1e-05
VMEM = pl.BlockSpec(memory_space=pltpu.VMEM)
LIMIT = 56 << 20

DEV = 16
BLK = 48
CH = 128
PACK = 8
GROUPS = BLK // PACK
LANES = PACK * BLK
TILES = LANES // 128
CPD = CH // DEV
ROWS = GROUPS * CPD
CROWS = GROUPS * DEV
N = DEV * BLK
STEP = 16
CELLS = STEP * BLK
NSTEP = BLK // STEP
SUMROWS = 64
PROWS = STEP // PACK * CPD
CPROWS = STEP // PACK * DEV
PN = STEP * DEV
NT = N // 128


def dot(a, b, ca=1, cb=0):
    return lax.dot_general(a, b, (((ca,), (cb,)), ((), ())), preferred_element_type=f32)


def mean(v):
    return jnp.mean(v, axis=-1, keepdims=True)


def normalize(values):
    values = values.astype(f32)
    centred = values - mean(values)
    inverse = lax.rsqrt(mean(centred * centred) + epsilon)
    return centred * inverse, inverse


def norm_back(scaled, normed, inverse):
    return inverse * (scaled - mean(scaled) - normed * mean(scaled * normed))


def to_channels(ref, values):
    halves = []
    for g in range(STEP // PACK):
        turned = values[g * LANES : (g + 1) * LANES].T
        halves.append(turned.reshape(DEV, CPD, LANES))
    ref[...] = jnp.concatenate(halves, axis=1).astype(bf16)[None]


def from_channels(ref):
    values = ref[0].astype(f32)
    parts = []
    for g in range(STEP // PACK):
        parts.append(values[:, g * CPD : (g + 1) * CPD, :].reshape(CH, LANES).T)
    return jnp.concatenate(parts, axis=0)


def mask_of(rmask, axis):
    first = lax.axis_index(axis) * BLK
    lane = lax.broadcasted_iota(jnp.int32, (BLK, N), 1)
    sub = lax.broadcasted_iota(jnp.int32, (BLK, N), 0)
    picked = jnp.where(lane == sub + first, rmask[...].astype(f32), 0.0)
    return jnp.broadcast_to(jnp.sum(picked, axis=1, keepdims=True), (BLK, CH))


def front_kernel(
    pm, sp, ct, rmask, lg, lb, og, ob, wa, wag, wb, wbg, wg, wo,
    gx_t, fa_t, fb_t, a1, a2, b1, b2, gg, gwo, gvec, rm, km,
):
    step = pl.program_id(0)

    @pl.when(step == 0)
    def _():
        rm[...] = mask_of(rmask, "row")
        km[...] = mask_of(rmask, "col")

    rows = rm[pl.ds(pl.multiple_of(step * STEP, STEP), STEP), :]
    mask = jnp.broadcast_to(rows[:, None, :] * km[...][None], (STEP, BLK, CH)).reshape(CELLS, CH)
    hat, _ = normalize(pm[...].reshape(CELLS, CH))
    zn = (hat * lg[...] + lb[...]).astype(bf16)
    ohat, oinv = normalize(sp[...].reshape(CELLS, CH))
    xn = (ohat * og[...] + ob[...]).astype(bf16)
    gate = jax.nn.sigmoid(dot(zn, wg[...]))
    update = dot(xn, wo[...])
    up = ct[...].reshape(CELLS, CH).astype(f32) * gate
    gu = up.astype(bf16)
    gg[...] = (up * update * (1.0 - gate)).astype(bf16)
    gxn = dot(gu, wo[...], 1, 1)
    to_channels(gx_t, norm_back(gxn * og[...], ohat, oinv))
    sig_a = jax.nn.sigmoid(dot(zn, wag[...]))
    ma = mask * sig_a
    fa = ma * dot(zn, wa[...])
    a1[...] = ma
    a2[...] = fa * (1.0 - sig_a)
    to_channels(fa_t, fa)
    sig_b = jax.nn.sigmoid(dot(zn, wbg[...]))
    mb = mask * sig_b
    fb = mb * dot(zn, wb[...])
    b1[...] = mb
    b2[...] = fb * (1.0 - sig_b)
    to_channels(fb_t, fb)
    gw = dot(xn, gu, 0, 0)
    sums = jnp.concatenate(
        [
            jnp.sum(gxn * ohat, axis=0, keepdims=True),
            jnp.sum(gxn, axis=0, keepdims=True),
            jnp.zeros((6, CH), f32),
        ],
        axis=0,
    )

    @pl.when(step == 0)
    def _():
        gwo[...] = gw
        gvec[...] = sums

    @pl.when(step > 0)
    def _():
        gwo[...] += gw
        gvec[...] += sums


def whole(*shape):
    return pl.BlockSpec(shape, lambda i: (0,) * len(shape))


def specs():
    cells = pl.BlockSpec((STEP, BLK, CH), lambda i: (i, 0, 0))
    flat = pl.BlockSpec((CELLS, CH), lambda i: (i, 0))
    turned = pl.BlockSpec((1, DEV, PROWS, LANES), lambda i: (i, 0, 0, 0))
    return cells, flat, turned


TURNED = jax.ShapeDtypeStruct((NSTEP, DEV, PROWS, LANES), bf16)


def front(pm, sp, ct, rmask, vecs, weights):
    cells, flat, turned = specs()
    c_shape = jax.ShapeDtypeStruct((BLK * BLK, CH), f32)
    return pl.pallas_call(
        front_kernel,
        grid=(NSTEP,),
        in_specs=[cells] * 3 + [whole(1, N)] + [whole(1, CH)] * 4 + [whole(CH, CH)] * 6,
        out_specs=[turned] * 3 + [flat] * 5 + [whole(CH, CH), whole(8, CH)],
        out_shape=[TURNED] * 3
        + [c_shape] * 4
        + [
            jax.ShapeDtypeStruct((BLK * BLK, CH), bf16),
            jax.ShapeDtypeStruct((CH, CH), f32),
            jax.ShapeDtypeStruct((8, CH), f32),
        ],
        scratch_shapes=[pltpu.VMEM((BLK, CH), f32)] * 2,
        name="front",
        compiler_params=pltpu.CompilerParams(vmem_limit_bytes=LIMIT),
    )(pm, sp, ct, rmask, *vecs, *weights)


def back_kernel(
    pm, gfa, gfb, a1, a2, b1, b2, gg, lg, lb, wa, wag, wb, wbg, wg, gp, gw, gvec, wcat
):
    step = pl.program_id(0)

    @pl.when(step == 0)
    def _():
        for k, w in enumerate((wa, wag, wb, wbg, wg)):
            wcat[:, k * CH : (k + 1) * CH] = w[...]

    hat, inv = normalize(pm[...].reshape(CELLS, CH))
    zn = (hat * lg[...] + lb[...]).astype(bf16)
    ga = from_channels(gfa)
    gb = from_channels(gfb)
    grads = jnp.concatenate(
        [
            (ga * a1[...]).astype(bf16),
            (ga * a2[...]).astype(bf16),
            (gb * b1[...]).astype(bf16),
            (gb * b2[...]).astype(bf16),
            gg[...],
        ],
        axis=1,
    )
    gz = dot(grads, wcat[...], 1, 1)
    gp[...] = norm_back(gz * lg[...], hat, inv).astype(bf16).reshape(STEP, BLK, CH)
    part = dot(zn, grads, 0, 0)
    sums = jnp.concatenate(
        [
            jnp.sum(gz * hat, axis=0, keepdims=True),
            jnp.sum(gz, axis=0, keepdims=True),
            jnp.zeros((6, CH), f32),
        ],
        axis=0,
    )

    @pl.when(step == 0)
    def _():
        gw[...] = part
        gvec[...] = sums

    @pl.when(step > 0)
    def _():
        gw[...] += part
        gvec[...] += sums


def back(pm, gfa, gfb, a1, a2, b1, b2, gg, vecs, weights):
    cells, flat, turned = specs()
    return pl.pallas_call(
        back_kernel,
        grid=(NSTEP,),
        in_specs=[cells, turned, turned]
        + [flat] * 5
        + [whole(1, CH)] * 2
        + [whole(CH, CH)] * 5,
        out_specs=[cells, whole(CH, 5 * CH), whole(8, CH)],
        out_shape=[
            jax.ShapeDtypeStruct((BLK, BLK, CH), bf16),
            jax.ShapeDtypeStruct((CH, 5 * CH), f32),
            jax.ShapeDtypeStruct((8, CH), f32),
        ],
        scratch_shapes=[pltpu.VMEM((CH, 5 * CH), bf16)],
        name="back",
        compiler_params=pltpu.CompilerParams(vmem_limit_bytes=LIMIT),
    )(pm, gfa, gfb, a1, a2, b1, b2, gg, *vecs, *weights)


def peer(axis, d):
    return lax.rem(lax.axis_index(axis) + d, DEV)


def greet(axes):
    barrier = pltpu.get_barrier_semaphore()
    for axis in axes:

        def hello(d, carry):
            pl.semaphore_signal(
                barrier, inc=1, device_id={axis: peer(axis, d)}, device_id_type=MESH
            )
            return carry

        lax.fori_loop(1, DEV, hello, 0)
    pl.semaphore_wait(barrier, len(axes) * (DEV - 1))


def each(action):
    def run(d, carry):
        action(d)
        return carry

    lax.fori_loop(1, DEV, run, 0)


def copier(axis, src, dst, send, recv):
    def make(d):
        t = peer(axis, d)
        return pltpu.make_async_remote_copy(
            src_ref=src(t),
            dst_ref=dst,
            send_sem=send.at[d],
            recv_sem=recv.at[d],
            device_id={axis: t},
            device_id_type=MESH,
        )

    return make


def span(count, action, start=0):
    def run(d, carry):
        action(d)
        return carry

    lax.fori_loop(start, count, run, 0)


def arrive(ref, sem):
    pltpu.make_async_copy(ref, ref, sem).wait()


def push(src, dst, send, recv, axis, t):
    pltpu.make_async_remote_copy(
        src_ref=src,
        dst_ref=dst,
        send_sem=send,
        recv_sem=recv,
        device_id={axis: t},
        device_id_type=MESH,
    ).start()


def keep(src, dst, sem):
    pltpu.make_async_copy(src, dst, sem).start()


def assemble(src, scr, dst, first):
    for a in range(PACK):
        rows = jnp.concatenate(
            [src[q][:, a * BLK : (a + 1) * BLK].astype(f32) for q in range(DEV)], axis=1
        )
        for t in range(NT):
            scr[t, pl.ds(a, CPROWS, stride=PACK), :] = rows[:, t * 128 : (t + 1) * 128]
    for t in range(NT):
        dst[first : first + PN, t * 128 : (t + 1) * 128] = scr[t].astype(bf16)


def turn_order():
    lane = lax.broadcasted_iota(jnp.int32, (N, N), 1)
    sub = lax.broadcasted_iota(jnp.int32, (N, N), 0)
    piece = lane >> 8
    place = ((lane >> 4) & 15) * BLK + piece * STEP + (lane & 15)
    return jnp.where(place == sub, 1.0, 0.0).astype(bf16)


def tri_kernel(
    gx, fa, fb, ga, gb,
    rbuf, scr, sbuf, gq, fq, asm, gn, left, order, fn, acc, dis, cbuf, hbuf,
    r_send, r_recv, g_send, g_recv, x_send, x_recv, f_send, f_recv,
    c_send, c_recv, h_send, h_recv,
):
    row, col = lax.axis_index("row"), lax.axis_index("col")
    odd = lax.rem(col, 2)
    sibling = col + 1 - 2 * odd
    arrays = (gx, fb, fa)
    outs = (ga, gb)
    greet(("row", "col"))
    for a in range(3):
        for p in range(NSTEP):
            keep(arrays[a].at[p, row], rbuf.at[a, p, row], r_recv.at[a, p])

            def send(d, a=a, p=p):
                t = peer("row", d)
                push(
                    arrays[a].at[p, t], rbuf.at[a, p, row], r_send.at[a], r_recv.at[a, p], "row", t
                )

            span(DEV, send, 1)
    order[...] = turn_order()

    def shuffle(a, p):
        arrive(rbuf.at[a, p], r_recv.at[a, p])
        for t in range(TILES):
            lanes = slice(t * 128, (t + 1) * 128)
            scr[t] = rbuf[a, p, :, :, lanes].reshape(DEV * PROWS, 128).astype(f32)
            for m in range(CPD):
                sbuf[a, p, m, :, lanes] = scr[t, pl.ds(m, CPROWS, stride=CPD), :].astype(bf16)

    HALF = CPROWS // 2

    def half(h):
        return pl.ds(pl.multiple_of(h * HALF, HALF), HALF)

    for p in range(NSTEP):
        shuffle(0, p)
        keep(sbuf.at[0, p, col // 2, half(odd)], gq.at[p, col, half(odd)], g_recv.at[p])

        def send(d, p=p):
            t = peer("col", d)
            h = half(lax.rem(t, 2))
            push(sbuf.at[0, p, t // 2, h], gq.at[p, col, h], g_send, g_recv.at[p], "col", t)

        span(DEV, send, 1)

    def factor(a, p):
        shuffle(a, p)
        same = odd == a - 1

        @pl.when(same)
        def _():
            keep(sbuf.at[a, p, col // 2], fq.at[p, col], f_recv.at[p])

        def send(d):
            t = lax.rem(col + 2 * d + jnp.where(same, 0, 1), DEV)
            push(sbuf.at[a, p, t // 2], fq.at[p, col], f_send, f_recv.at[p], "col", t)

        span(DEV // 2, send, jnp.where(same, 1, 0))

    factor(1, 0)
    for p in range(NSTEP):
        arrive(gq.at[p, :, half(odd)], g_recv.at[p])
        push(
            gq.at[p, :, half(odd)],
            gq.at[p, :, half(odd)],
            x_send.at[p],
            x_recv.at[p],
            "col",
            sibling,
        )
    factor(1, 1)
    factor(1, 2)
    for p in range(NSTEP):
        arrive(gq.at[p, :, half(1 - odd)], x_recv.at[p])
        assemble(gq.at[p], asm, gn, p * PN)

    @pl.when(odd == 0)
    def _():
        left[...] = dot(gn[...], order[...]).astype(bf16)

    @pl.when(odd == 1)
    def _():
        left[...] = dot(order[...], gn[...], 0, 1).astype(bf16)

    factor(2, 0)

    def multiply():
        for p in range(NSTEP):
            arrive(fq.at[p], f_recv.at[p])
            assemble(fq.at[p], asm, fn, 0)
            values = dot(left[:, p * PN : (p + 1) * PN], fn[...])
            for t in range(NT):
                lanes = values[:, t * 128 : (t + 1) * 128]
                if p == 0:
                    acc[t] = lanes
                else:
                    acc[t] += lanes
        for p in range(NSTEP):
            rows = [
                [acc[t, pl.ds(p * PN + a, CPROWS, stride=PACK), :] for t in range(NT)]
                for a in range(PACK)
            ]

            def piece(a, q):
                lo, hi = q * BLK, (q + 1) * BLK
                first, last = lo // 128, (hi - 1) // 128
                if first == last:
                    return rows[a][first][:, lo - first * 128 : hi - first * 128]
                return jnp.concatenate(
                    [rows[a][first][:, lo - first * 128 :], rows[a][last][:, : hi - last * 128]],
                    axis=1,
                )

            for q in range(DEV):
                dis[p, q] = jnp.concatenate([piece(a, q) for a in range(PACK)], axis=1).astype(bf16)
            keep(dis.at[p, col], cbuf.at[p, col], c_recv.at[odd, p])

            def send(d):
                t = peer("col", d)
                push(dis.at[p, t], cbuf.at[p, col], c_send, c_recv.at[odd, p], "col", t)

            span(DEV, send, 1)

    pl.when(odd == 0)(multiply)
    factor(2, 1)
    factor(2, 2)
    pl.when(odd == 1)(multiply)

    for h in range(2):
        for p in range(NSTEP):
            arrive(cbuf.at[p, 0 : DEV // 2], c_recv.at[h, p])
            for t in range(TILES):
                lanes = slice(t * 128, (t + 1) * 128)
                for m in range(CPD):
                    scr[t, pl.ds(m, CPROWS, stride=CPD), :] = cbuf[p, 2 * m + h, :, lanes].astype(
                        f32
                    )
                hbuf[h, p, :, :, lanes] = scr[t].reshape(DEV, PROWS, 128).astype(bf16)
            keep(hbuf.at[h, p, row], outs[h].at[p, row], h_recv.at[h, p])

            def send(d, h=h, p=p):
                t = peer("row", d)
                push(hbuf.at[h, p, t], outs[h].at[p, row], h_send, h_recv.at[h, p], "row", t)

            span(DEV, send, 1)

    for h in range(2):
        for p in range(NSTEP):
            arrive(outs[h].at[p], h_recv.at[h, p])
    for a in range(3):
        arrive(rbuf.at[a, :, 0 : DEV - 1], r_send.at[a])
    arrive(gq.at[:, 0 : DEV - 1, 0:HALF], g_send)
    for p in range(NSTEP):
        arrive(gq.at[p, :, 0:HALF], x_send.at[p])
    arrive(fq.at[:, 0 : DEV - 1], f_send)
    arrive(cbuf.at[:, 0 : DEV - 1], c_send)
    arrive(hbuf.at[:, :, 0 : DEV - 1], h_send)


def tri(gx, fa, fb):
    dma = pltpu.SemaphoreType.DMA
    turned = (NSTEP, DEV, PROWS, LANES)
    crossed = (NSTEP, DEV, CPROWS, LANES)
    return pl.pallas_call(
        tri_kernel,
        in_specs=[VMEM] * 3,
        out_specs=[VMEM] * 2,
        out_shape=[TURNED] * 2,
        scratch_shapes=[
            pltpu.VMEM((3,) + turned, bf16),
            pltpu.VMEM((TILES, DEV * PROWS, 128), f32),
            pltpu.VMEM((3, NSTEP, CPD, CPROWS, LANES), bf16),
            pltpu.VMEM(crossed, bf16),
            pltpu.VMEM(crossed, bf16),
            pltpu.VMEM((NT, PN, 128), f32),
            pltpu.VMEM((N, N), bf16),
            pltpu.VMEM((N, N), bf16),
            pltpu.VMEM((N, N), bf16),
            pltpu.VMEM((PN, N), bf16),
            pltpu.VMEM((NT, N, 128), f32),
            pltpu.VMEM(crossed, bf16),
            pltpu.VMEM(crossed, bf16),
            pltpu.VMEM((2,) + turned, bf16),
            dma((3,)),
            dma((3, NSTEP)),
            dma,
            dma((NSTEP,)),
            dma((NSTEP,)),
            dma((NSTEP,)),
            dma,
            dma((NSTEP,)),
            dma,
            dma((2, NSTEP)),
            dma,
            dma((2, NSTEP)),
        ],
        name="tri",
        compiler_params=pltpu.CompilerParams(
            collective_id=1, has_side_effects=True, vmem_limit_bytes=LIMIT
        ),
    )(gx, fa, fb)


def sum_kernel(gw, gwo, gvec, lvec, out, part, got1, mid, got2, fin, sem_s, sem_r, loc):
    row, col = lax.axis_index("row"), lax.axis_index("col")
    for k in range(5):
        for j in range(2):
            part[2 * k + j] = gw[j * 64 : (j + 1) * 64, k * CH : (k + 1) * CH].astype(bf16)
    for j in range(2):
        part[10 + j] = gwo[j * 64 : (j + 1) * 64, :].astype(bf16)
    part[12] = jnp.concatenate(
        [lvec[...], gvec[...], jnp.zeros((SUMROWS - 16, CH), f32)], axis=0
    ).astype(bf16)
    part[13:16] = jnp.zeros((3, SUMROWS, CH), bf16)
    own = pltpu.make_async_copy(part.at[col], got1.at[col], loc.at[0])
    own.start()
    greet(("row", "col"))
    one = copier("col", lambda t: part.at[t], got1.at[col], sem_s.at[0], sem_r.at[0])
    each(lambda d: one(d).start())
    own.wait()
    each(lambda d: one(d).wait())
    mid[...] = jnp.sum(got1[...].astype(f32), axis=0).astype(bf16)
    own = pltpu.make_async_copy(mid, got2.at[row], loc.at[1])
    own.start()
    two = copier("row", lambda t: mid, got2.at[row], sem_s.at[1], sem_r.at[1])
    each(lambda d: two(d).start())
    own.wait()
    each(lambda d: two(d).wait())
    fin[...] = (jnp.sum(got2[...].astype(f32), axis=0) * (1.0 / N)).astype(bf16)
    own = pltpu.make_async_copy(fin, out.at[col], loc.at[2])
    own.start()
    three = copier("col", lambda t: fin, out.at[col], sem_s.at[2], sem_r.at[2])
    each(lambda d: three(d).start())
    own.wait()
    each(lambda d: three(d).wait())


def sum_all(gw, gwo, gvec, lvec):
    dma = pltpu.SemaphoreType.DMA
    wide = (DEV, SUMROWS, CH)
    return pl.pallas_call(
        sum_kernel,
        in_specs=[VMEM] * 4,
        out_specs=VMEM,
        out_shape=jax.ShapeDtypeStruct(wide, bf16),
        scratch_shapes=[
            pltpu.VMEM(wide, bf16),
            pltpu.VMEM(wide, bf16),
            pltpu.VMEM((SUMROWS, CH), bf16),
            pltpu.VMEM(wide, bf16),
            pltpu.VMEM((SUMROWS, CH), bf16),
            dma((3, DEV)),
            dma((3, DEV)),
            dma((3,)),
        ],
        name="sum_all",
        compiler_params=pltpu.CompilerParams(
            collective_id=3, has_side_effects=True, vmem_limit_bytes=LIMIT
        ),
    )(gw, gwo, gvec, lvec)


def finish_kernel(s, *outs):
    for k in range(6):
        for j in range(2):
            outs[k][j * 64 : (j + 1) * 64, :] = s[2 * k + j].astype(f32)
    vec = s[12].astype(f32)
    outs[6][...] = vec[0:1]
    outs[7][...] = vec[1:2]
    outs[8][...] = vec[8:9]
    outs[9][...] = vec[9:10]


def finish(s):
    return pl.pallas_call(
        finish_kernel,
        in_specs=[VMEM],
        out_specs=[VMEM] * 10,
        out_shape=[jax.ShapeDtypeStruct((CH, CH), f32)] * 6
        + [jax.ShapeDtypeStruct((1, CH), f32)] * 4,
        name="finish",
    )(s)


def body(
    pair_map,
    saved_product,
    cotangent,
    residue_mask,
    ln_gain,
    ln_bias,
    out_gain,
    out_bias,
    w_a,
    w_ag,
    w_b,
    w_bg,
    w_g,
    w_o,
):
    vecs = [v.reshape(1, CH) for v in (ln_gain, ln_bias, out_gain, out_bias)]
    weights = [w_a, w_ag, w_b, w_bg, w_g, w_o]
    gx, fa, fb, a1, a2, b1, b2, gg, gwo, gvec = front(
        pair_map, saved_product, cotangent, residue_mask.reshape(1, N), vecs, weights
    )
    gfa, gfb = tri(gx, fa, fb)
    grad_pair, gw, lvec = back(
        pair_map, gfa, gfb, a1, a2, b1, b2, gg, vecs[:2], weights[:5]
    )
    outs = finish(sum_all(gw, gwo, gvec, lvec))
    return (grad_pair,) + tuple(outs[:6]) + tuple(v.reshape(CH) for v in outs[6:])


def solution(mesh):
    return jax.shard_map(
        body,
        mesh=mesh,
        in_specs=(P("row", "col", None),) * 3 + (P(),) * 11,
        out_specs=(P("row", "col", None),) + (P(),) * 10,
        check_vma=False,
    )
```

time: 190 us -> 141 us (0.74)
  Pallas kernels: 181 us -> 139 us
  local copies, waits for them, and re-layouts: 7.18 us -> 1.27 us
    pallas_call x4 -> x2, Pallas kernels: 143 us -> 99.9 us  [the longest x1 92.8 us: tri(): pl.pallas_call(tri_kernel, in_specs=[VMEM] * 3, out_specs=[VMEM] * 2, out...]
    unnamed x6 -> x0, local copies, waits for them, and re-layouts: 3.74 us -> none
    concatenate x2 -> x0, local copies, waits for them, and re-layouts: 2.08 us -> none  [the longest x1 1.31 us: body(): jnp.concatenate([jnp.stack([ln_gain, ln_bias, out_gain, out_bias]), jnp.z...]
where the time goes in v2:
time: 141 us
  Pallas kernels  139 us (99%)
    pallas_call x1, Pallas kernels, tri(): pl.pallas_call(tri_kernel, in_specs=[VMEM] * 3, out_specs=[VMEM] * 2, out...  92.8 us
    pallas_call x1, Pallas kernels, sum_all(): pl.pallas_call(sum_kernel, in_specs=[VMEM] * 4, out_specs=VMEM, out_shape...  30.6 us
    pallas_call x1, Pallas kernels, front(): pl.pallas_call(front_kernel, grid=(NSTEP,), in_specs=[cells] * 3 + [whole...  7.12 us
    pallas_call x1, Pallas kernels, back(): pl.pallas_call(back_kernel, grid=(NSTEP,), in_specs=[cells, turned, turne...  6.53 us

profile of v2, /device:TPU:1, one launch (start us, length us, event | category | flops | bytes accessed | tf_op | source)
XLA Modules:
  0.0 140.8 jit_solution(8569614697078529413)
XLA Ops:
  0.6 1.3 reshape.49.rmask
  1.9 7.1 %front.1 = (bf16[3,16,16,384]{3,2,1,0:T(8,128)(2,1)}, bf16[3,16,16,384]{3,2,1,0:T(8,128)(2,1)}, bf16[3,16,16,384]{3,2,1,0:T(8,128)(2,1)}, f32[2304,128]{1,0:T(8,...) custom-call(bf16[48,48,128]{2,1,0:T(8,128)(2,1)} %pm.3, ...), custom_call_target="tpu_custom_call" | custom-call | tf_op jit(solution)/shard_map/front/pallas_call | solution.py:153
  9.0 92.8 %tri.1 = (bf16[3,16,16,384]{3,2,1,0:T(8,128)(2,1)}, bf16[3,16,16,384]{3,2,1,0:T(8,128)(2,1)}) custom-call(bf16[3,16,16,384]{3,2,1,0:T(8,128)(2,1)} %get-tuple-element.36.gx, bf16[3,16,16,384]{3,2,1,0:T(8,128)(2,1)} %get-tuple-element.37.fa, bf16[3,16,16,384]{3,2,1,0:T(8,128)(2,1)} %get-tuple-element.38.fb), custom_call_target="tpu_custom_call" | custom-call | tf_op jit(solution)/shard_map/tri/pallas_call | solution.py:493
  101.8 6.5 %back.1 = (bf16[48,48,128]{2,1,0:T(8,128)(2,1)}, f32[128,640]{1,0:T(8,128)}, f32[8,128]{1,0:T(8,128)}) custom-call(bf16[48,48,128]{2,1,0:T(8,128)(2,1)} %pm.3, bf16[3,16,16,384]{3,2,1,0:T(8,128)(2,1)} %get-tuple-element.39.gfa, bf16[3,16,16,384]{3,2,1,0:T(8,128)(2,1)} %get-tuple-element.40.gfb, f32[2304,128]{1,0:T(8,128)} %get-tuple-element.41.a1, ...), custom_call_target="tpu_custom_call" | custom-call | tf_op jit(solution)/shard_map/back/pallas_call | solution.py:220
  108.4 30.6 %sum_all.1.s = bf16[16,64,128]{2,1,0:T(8,128)(2,1)} custom-call(f32[128,640]{1,0:T(8,128)} %get-tuple-element.47.gw, f32[128,128]{1,0:T(8,128)} %get-tuple-element.48.gwo, f32[8,128]{1,0:T(8,128)} %get-tuple-element.49.gvec, f32[8,128]{1,0:T(8,128)} %get-tuple-element.50.lvec), custom_call_target="tpu_custom_call" | custom-call | tf_op jit(solution)/shard_map/sum_all/pallas_call | solution.py:570
  139.0 1.7 %finish.1 = (f32[128,128]{1,0:T(8,128)}, f32[128,128]{1,0:T(8,128)}, f32[128,128]{1,0:T(8,128)}, f32[128,128]{1,0:T(8,128)}, f32[128,128]{1,0:T(8,128)}, /*index...) custom-call(bf16[16,64,128]{2,1,0:T(8,128)(2,1)} %sum_all.1.s), custom_call_target="tpu_custom_call" | custom-call | tf_op jit(solution)/shard_map/finish/pallas_call | solution.py:604

commit v3 on v2

v3 whole, which is shorter than its diff:
```python
import jax
import jax.numpy as jnp
from jax import lax
from jax.experimental import pallas as pl
from jax.experimental.pallas import tpu as pltpu
from jax.sharding import PartitionSpec as P

MESH = pl.DeviceIdType.MESH
f32 = jnp.float32
bf16 = jnp.bfloat16
epsilon = 1e-05
VMEM = pl.BlockSpec(memory_space=pltpu.VMEM)
LIMIT = 56 << 20

DEV = 16
BLK = 48
CH = 128
PACK = 8
GROUPS = BLK // PACK
LANES = PACK * BLK
TILES = LANES // 128
CPD = CH // DEV
ROWS = GROUPS * CPD
CROWS = GROUPS * DEV
N = DEV * BLK
STEP = 16
CELLS = STEP * BLK
NSTEP = BLK // STEP
EARLY = 4 * CH // DEV
LATE = 2 * CH // DEV
PROWS = STEP // PACK * CPD
CPROWS = STEP // PACK * DEV
PN = STEP * DEV
NT = N // 128
ODD = 11


def dot(a, b, ca=1, cb=0):
    return lax.dot_general(a, b, (((ca,), (cb,)), ((), ())), preferred_element_type=f32)


def mean(v):
    return jnp.mean(v, axis=-1, keepdims=True)


def normalize(values):
    values = values.astype(f32)
    centred = values - mean(values)
    inverse = lax.rsqrt(mean(centred * centred) + epsilon)
    return centred * inverse, inverse


def norm_back(scaled, normed, inverse):
    return inverse * (scaled - mean(scaled) - normed * mean(scaled * normed))


def to_channels(ref, values):
    halves = []
    for g in range(STEP // PACK):
        turned = values[g * LANES : (g + 1) * LANES].T
        halves.append(turned.reshape(DEV, CPD, LANES))
    ref[...] = jnp.concatenate(halves, axis=1).astype(bf16)


def from_channels(ref):
    values = ref[...].astype(f32)
    parts = []
    for g in range(STEP // PACK):
        parts.append(values[:, g * CPD : (g + 1) * CPD, :].reshape(CH, LANES).T)
    return jnp.concatenate(parts, axis=0)


def add_to(ref, values, first):
    if first:
        ref[...] = values
    else:
        ref[...] += values


def column_sum(values):
    return jnp.sum(values, axis=0, keepdims=True)


def mask_of(rmask, axis):
    first = lax.axis_index(axis) * BLK
    lane = lax.broadcasted_iota(jnp.int32, (BLK, N), 1)
    sub = lax.broadcasted_iota(jnp.int32, (BLK, N), 0)
    picked = jnp.where(lane == sub + first, rmask[...].astype(f32), 0.0)
    return jnp.broadcast_to(jnp.sum(picked, axis=1, keepdims=True), (BLK, CH))


def peer(axis, d):
    return lax.axis_index(axis) ^ d


def span(count, action, start=0):
    def run(d, carry):
        action(d)
        return carry

    lax.fori_loop(start, count, run, 0)


def arrive(ref, sem):
    pltpu.make_async_copy(ref, ref, sem).wait()


def push(src, dst, send, recv, axis, t):
    pltpu.make_async_remote_copy(
        src_ref=src,
        dst_ref=dst,
        send_sem=send,
        recv_sem=recv,
        device_id={axis: t},
        device_id_type=MESH,
    ).start()


def keep(src, dst, sem):
    pltpu.make_async_copy(src, dst, sem).start()


def scatter(axis, src, dst, send, recv):
    me = lax.axis_index(axis)
    keep(src(me), dst.at[me], recv)

    def go(d):
        t = peer(axis, (d * ODD) & (DEV - 1))
        push(src(t), dst.at[me], send, recv, axis, t)

    span(DEV, go, 1)


def assemble(src, scr, dst, first):
    for a in range(PACK):
        rows = jnp.concatenate(
            [src[q][:, a * BLK : (a + 1) * BLK].astype(f32) for q in range(DEV)], axis=1
        )
        for t in range(NT):
            scr[t, pl.ds(a, CPROWS, stride=PACK), :] = rows[:, t * 128 : (t + 1) * 128]
    for t in range(NT):
        dst[first : first + PN, t * 128 : (t + 1) * 128] = scr[t].astype(bf16)


def turn_order():
    lane = lax.broadcasted_iota(jnp.int32, (N, N), 1)
    sub = lax.broadcasted_iota(jnp.int32, (N, N), 0)
    piece = lane >> 8
    place = ((lane >> 4) & 15) * BLK + piece * STEP + (lane & 15)
    return jnp.where(place == sub, 1.0, 0.0).astype(bf16)


def kernel(
    pm, sp, ct, rmask, lg, lb, og, ob, wa, wag, wb, wbg, wg, wo,
    gp, eout, lout, vout,
    zn, hat, inv, a1, a2, b1, b2, gg, gz, gwo, gwa, gwb, lvec, wcat, tx, rx,
    rbuf, scr, sbuf, gq, fq, asm, gn, left, order, fn, acc, dis, cbuf, hbuf,
    epart, eg1, emid, eg2, efin, lpart, lg1, lmid, lg2, lfin,
    r_send, r_recv, g_send, g_recv, x_send, x_recv, f_send, f_recv,
    c_send, c_recv, h_send, h_recv, e_send, e_recv, l_send, l_recv,
):
    row, col = lax.axis_index("row"), lax.axis_index("col")
    odd = lax.rem(col, 2)
    sibling = col + 1 - 2 * odd
    barrier = pltpu.get_barrier_semaphore()
    for axis in ("row", "col"):

        def hello(d, axis=axis):
            pl.semaphore_signal(
                barrier, inc=1, device_id={axis: peer(axis, d)}, device_id_type=MESH
            )

        span(DEV, hello, 1)

    lvec[...] = jnp.zeros((8, CH), f32)
    rm = mask_of(rmask, "row")
    km = mask_of(rmask, "col")
    for k, w in enumerate((wa, wag, wg, wb, wbg)):
        wcat[:, k * CH : (k + 1) * CH] = w[...]

    def cells(p):
        return slice(p * CELLS, (p + 1) * CELLS)

    def rows_of(p):
        return slice(p * STEP, (p + 1) * STEP)

    def launch(a, p):
        scatter("row", lambda t: tx.at[a, p, t], rbuf.at[a, p], r_send.at[a], r_recv.at[a, p])

    for p in range(NSTEP):
        here = cells(p)
        phat, pinv = normalize(pm[rows_of(p)].reshape(CELLS, CH))
        hat[here] = phat
        inv[here] = jnp.broadcast_to(pinv, (CELLS, CH))
        znp = (phat * lg[...] + lb[...]).astype(bf16)
        zn[here] = znp
        ohat, oinv = normalize(sp[rows_of(p)].reshape(CELLS, CH))
        xn = (ohat * og[...] + ob[...]).astype(bf16)
        gate = jax.nn.sigmoid(dot(znp, wg[...]))
        up = ct[rows_of(p)].reshape(CELLS, CH).astype(f32) * gate
        gu = up.astype(bf16)
        gxn = dot(gu, wo[...], 1, 1)
        to_channels(tx.at[0, p], norm_back(gxn * og[...], ohat, oinv))
        if p == 0:
            pl.semaphore_wait(barrier, 2 * (DEV - 1))
        launch(0, p)
        update = dot(xn, wo[...])
        gg[here] = (up * update * (1.0 - gate)).astype(bf16)
        add_to(gwo, dot(xn, gu, 0, 0), p == 0)
        add_to(lvec.at[2:3], column_sum(gxn * ohat), p == 0)
        add_to(lvec.at[3:4], column_sum(gxn), p == 0)

    for a, w, wgate, k1, k2 in ((1, wb, wbg, b1, b2), (2, wa, wag, a1, a2)):
        for p in range(NSTEP):
            here = cells(p)
            mask = jnp.broadcast_to(
                rm[rows_of(p)][:, None, :] * km[None], (STEP, BLK, CH)
            ).reshape(CELLS, CH)
            sig = jax.nn.sigmoid(dot(zn[here], wgate[...]))
            masked = mask * sig
            fac = masked * dot(zn[here], w[...])
            to_channels(tx.at[a, p], fac)
            launch(a, p)
            k1[here] = masked
            k2[here] = fac * (1.0 - sig)
    order[...] = turn_order()

    def shuffle(a, p):
        arrive(rbuf.at[a, p], r_recv.at[a, p])
        for t in range(TILES):
            lanes = slice(t * 128, (t + 1) * 128)
            scr[t] = rbuf[a, p, :, :, lanes].reshape(DEV * PROWS, 128).astype(f32)
            for m in range(CPD):
                sbuf[a, p, m, :, lanes] = scr[t, pl.ds(m, CPROWS, stride=CPD), :].astype(bf16)

    HALF = CPROWS // 2

    def half(h):
        return pl.ds(pl.multiple_of(h * HALF, HALF), HALF)

    for p in range(NSTEP):
        shuffle(0, p)
        keep(sbuf.at[0, p, col // 2, half(odd)], gq.at[p, col, half(odd)], g_recv.at[p])

        def send(d, p=p):
            t = peer("col", (d * ODD) & (DEV - 1))
            h = half(lax.rem(t, 2))
            push(sbuf.at[0, p, t // 2, h], gq.at[p, col, h], g_send, g_recv.at[p], "col", t)

        span(DEV, send, 1)

    def factor(a, p):
        shuffle(a, p)
        same = odd == a - 1

        @pl.when(same)
        def _():
            keep(sbuf.at[a, p, col // 2], fq.at[p, col], f_recv.at[p])

        def send(d):
            t = col ^ (2 * ((d * ODD) & (DEV // 2 - 1)) + jnp.where(same, 0, 1))
            push(sbuf.at[a, p, t // 2], fq.at[p, col], f_send, f_recv.at[p], "col", t)

        span(DEV // 2, send, jnp.where(same, 1, 0))

    factor(1, 0)
    for p in range(NSTEP):
        arrive(gq.at[p, :, half(odd)], g_recv.at[p])
        push(
            gq.at[p, :, half(odd)],
            gq.at[p, :, half(odd)],
            x_send.at[p],
            x_recv.at[p],
            "col",
            sibling,
        )
    factor(1, 1)
    factor(1, 2)
    for p in range(NSTEP):
        arrive(gq.at[p, :, half(1 - odd)], x_recv.at[p])
        assemble(gq.at[p], asm, gn, p * PN)

    @pl.when(odd == 0)
    def _():
        left[...] = dot(gn[...], order[...]).astype(bf16)

    @pl.when(odd == 1)
    def _():
        left[...] = dot(order[...], gn[...], 0, 1).astype(bf16)

    factor(2, 0)

    def multiply():
        for p in range(NSTEP):
            arrive(fq.at[p], f_recv.at[p])
            assemble(fq.at[p], asm, fn, 0)
            values = dot(left[:, p * PN : (p + 1) * PN], fn[...])
            for t in range(NT):
                lanes = values[:, t * 128 : (t + 1) * 128]
                if p == 0:
                    acc[t] = lanes
                else:
                    acc[t] += lanes
        for p in range(NSTEP):
            rows = [
                [acc[t, pl.ds(p * PN + a, CPROWS, stride=PACK), :] for t in range(NT)]
                for a in range(PACK)
            ]

            def piece(a, q):
                lo, hi = q * BLK, (q + 1) * BLK
                first, last = lo // 128, (hi - 1) // 128
                if first == last:
                    return rows[a][first][:, lo - first * 128 : hi - first * 128]
                return jnp.concatenate(
                    [rows[a][first][:, lo - first * 128 :], rows[a][last][:, : hi - last * 128]],
                    axis=1,
                )

            for q in range(DEV):
                dis[p, q] = jnp.concatenate([piece(a, q) for a in range(PACK)], axis=1).astype(bf16)
            scatter("col", lambda t: dis.at[p, t], cbuf.at[p], c_send, c_recv.at[odd, p])

    pl.when(odd == 0)(multiply)
    factor(2, 1)
    factor(2, 2)
    pl.when(odd == 1)(multiply)

    def relay(h, p):
        arrive(cbuf.at[p, 0 : DEV // 2], c_recv.at[h, p])
        for t in range(TILES):
            lanes = slice(t * 128, (t + 1) * 128)
            for m in range(CPD):
                scr[t, pl.ds(m, CPROWS, stride=CPD), :] = cbuf[p, 2 * m + h, :, lanes].astype(f32)
            hbuf[h, p, :, :, lanes] = scr[t].reshape(DEV, PROWS, 128).astype(bf16)
        scatter("row", lambda t: hbuf.at[h, p, t], rx.at[h, p], h_send, h_recv.at[h, p])

    for h in range(2):
        for p in range(NSTEP):
            relay(h, p)

    def grads_of(h, p, k1, k2):
        arrive(rx.at[h, p], h_recv.at[h, p])
        got = from_channels(rx.at[h, p])
        here = cells(p)
        return [(got * k1[here]).astype(bf16), (got * k2[here]).astype(bf16)]

    for p in range(NSTEP):
        here = cells(p)
        grads = jnp.concatenate(grads_of(0, p, a1, a2) + [gg[here]], axis=1)
        gz[here] = dot(grads, wcat[:, : 3 * CH], 1, 1)
        add_to(gwa, dot(zn[here], grads, 0, 0), p == 0)

    for t in range(DEV):
        k, at = divmod(t * EARLY, CH)
        source = gwo[at : at + EARLY, :] if k == 3 else gwa[at : at + EARLY, k * CH : (k + 1) * CH]
        epart[t] = source.astype(bf16)
    scatter("col", lambda t: epart.at[t], eg1, e_send.at[0], e_recv.at[0])

    def last(p):
        here = cells(p)
        grads = jnp.concatenate(grads_of(1, p, b1, b2), axis=1)
        total = gz[here] + dot(grads, wcat[:, 3 * CH :], 1, 1)
        add_to(gwb, dot(zn[here], grads, 0, 0), p == 0)
        add_to(lvec.at[0:1], column_sum(total * hat[here]), p == 0)
        add_to(lvec.at[1:2], column_sum(total), p == 0)
        return total

    def write(p, total):
        here = cells(p)
        value = norm_back(total * lg[...], hat[here], inv[here])
        gp[rows_of(p)] = value.astype(bf16).reshape(STEP, BLK, CH)

    write(0, last(0))
    arrive(eg1, e_recv.at[0])
    emid[...] = jnp.sum(eg1[...].astype(f32), axis=0).astype(bf16)
    scatter("row", lambda t: emid, eg2, e_send.at[1], e_recv.at[1])
    write(1, last(1))
    arrive(eg2, e_recv.at[1])
    efin[...] = (jnp.sum(eg2[...].astype(f32), axis=0) * (1.0 / N)).astype(bf16)
    scatter("col", lambda t: efin, eout, e_send.at[2], e_recv.at[2])
    total = last(2)

    vector = jnp.concatenate([lvec[...], jnp.zeros((8, CH), f32)], axis=0)
    for t in range(DEV):
        k, at = divmod(t * LATE, CH)
        source = gwb[at : at + LATE, k * CH : (k + 1) * CH]
        lpart[t] = jnp.concatenate([source, vector], axis=0).astype(bf16)
    scatter("col", lambda t: lpart.at[t], lg1, l_send.at[0], l_recv.at[0])
    write(2, total)
    arrive(lg1, l_recv.at[0])
    lmid[...] = jnp.sum(lg1[...].astype(f32), axis=0).astype(bf16)
    scatter("row", lambda t: lmid, lg2, l_send.at[1], l_recv.at[1])
    arrive(lg2, l_recv.at[1])
    done = jnp.sum(lg2[...].astype(f32), axis=0) * (1.0 / N)
    vout[...] = done[LATE:]
    lfin[...] = done[:LATE].astype(bf16)
    scatter("col", lambda t: lfin, lout, l_send.at[2], l_recv.at[2])

    for a in range(3):
        arrive(rbuf.at[a, :, 0 : DEV - 1], r_send.at[a])
    arrive(gq.at[:, 0 : DEV - 1, 0:HALF], g_send)
    for p in range(NSTEP):
        arrive(gq.at[p, :, 0:HALF], x_send.at[p])
    arrive(fq.at[:, 0 : DEV - 1], f_send)
    arrive(cbuf.at[:, 0 : DEV - 1], c_send)
    arrive(hbuf.at[:, :, 0 : DEV - 1], h_send)
    for k in range(3):
        arrive(eg1.at[0 : DEV - 1], e_send.at[k])
    arrive(lg1.at[0 : DEV - 1], l_send.at[0])
    arrive(lg2.at[0 : DEV - 1], l_send.at[1])
    arrive(lout.at[0 : DEV - 1], l_send.at[2])
    arrive(eout, e_recv.at[2])
    arrive(lout, l_recv.at[2])


def whole_step(*args):
    dma = pltpu.SemaphoreType.DMA
    turned = (NSTEP, DEV, PROWS, LANES)
    crossed = (NSTEP, DEV, CPROWS, LANES)
    flat = (BLK * BLK, CH)
    early = (DEV, EARLY, CH)
    late = (DEV, LATE + 16, CH)

    def wide(*shape):
        return pltpu.VMEM(shape, f32)

    def thin(*shape):
        return pltpu.VMEM(shape, bf16)

    return pl.pallas_call(
        kernel,
        in_specs=[VMEM] * 14,
        out_specs=[VMEM] * 4,
        out_shape=[
            jax.ShapeDtypeStruct((BLK, BLK, CH), bf16),
            jax.ShapeDtypeStruct(early, bf16),
            jax.ShapeDtypeStruct((DEV, LATE, CH), bf16),
            jax.ShapeDtypeStruct((16, CH), f32),
        ],
        scratch_shapes=[
            thin(*flat),
            wide(*flat),
            wide(*flat),
            wide(*flat),
            wide(*flat),
            wide(*flat),
            wide(*flat),
            thin(*flat),
            wide(*flat),
            wide(CH, CH),
            wide(CH, 3 * CH),
            wide(CH, 2 * CH),
            wide(8, CH),
            thin(CH, 5 * CH),
            thin(3, *turned),
            thin(2, *turned),
            thin(3, *turned),
            wide(TILES, DEV * PROWS, 128),
            thin(3, NSTEP, CPD, CPROWS, LANES),
            thin(*crossed),
            thin(*crossed),
            wide(NT, PN, 128),
            thin(N, N),
            thin(N, N),
            thin(N, N),
            thin(PN, N),
            wide(NT, N, 128),
            thin(*crossed),
            thin(*crossed),
            thin(2, *turned),
            thin(*early),
            thin(*early),
            thin(EARLY, CH),
            thin(*early),
            thin(EARLY, CH),
            thin(*late),
            thin(*late),
            thin(LATE + 16, CH),
            thin(*late),
            thin(LATE, CH),
            dma((3,)),
            dma((3, NSTEP)),
            dma,
            dma((NSTEP,)),
            dma((NSTEP,)),
            dma((NSTEP,)),
            dma,
            dma((NSTEP,)),
            dma,
            dma((2, NSTEP)),
            dma,
            dma((2, NSTEP)),
            dma((3,)),
            dma((3,)),
            dma((3,)),
            dma((3,)),
        ],
        name="whole_step",
        compiler_params=pltpu.CompilerParams(
            collective_id=1, has_side_effects=True, vmem_limit_bytes=LIMIT
        ),
    )(*args)


def finish_kernel(pair, early, late, vec, *outs):
    outs[0][...] = pair[...]
    place = (1, 2, 5, 6)
    for t in range(DEV):
        k, at = divmod(t * EARLY, CH)
        outs[place[k]][at : at + EARLY, :] = early[t].astype(f32)
        k, at = divmod(t * LATE, CH)
        outs[3 + k][at : at + LATE, :] = late[t].astype(f32)
    for k in range(4):
        outs[7 + k][...] = vec[k : k + 1]


def finish(*args):
    return pl.pallas_call(
        finish_kernel,
        in_specs=[VMEM] * 4,
        out_specs=[VMEM] * 11,
        out_shape=[jax.ShapeDtypeStruct((BLK, BLK, CH), bf16)]
        + [jax.ShapeDtypeStruct((CH, CH), f32)] * 6
        + [jax.ShapeDtypeStruct((1, CH), f32)] * 4,
        name="finish",
    )(*args)


def body(
    pair_map,
    saved_product,
    cotangent,
    residue_mask,
    ln_gain,
    ln_bias,
    out_gain,
    out_bias,
    *weights,
):
    vecs = [v.reshape(1, CH) for v in (ln_gain, ln_bias, out_gain, out_bias)]
    outs = finish(
        *whole_step(
            pair_map, saved_product, cotangent, residue_mask.reshape(1, N), *vecs, *weights
        )
    )
    return tuple(outs[:7]) + tuple(v.reshape(CH) for v in outs[7:])


def solution(mesh):
    return jax.shard_map(
        body,
        mesh=mesh,
        in_specs=(P("row", "col", None),) * 3 + (P(),) * 11,
        out_specs=(P("row", "col", None),) + (P(),) * 10,
        check_vma=False,
    )
```

time: 141 us -> 119 us (0.84)
  Pallas kernels: 139 us -> 117 us
    pallas_call x5 -> x2, Pallas kernels: 139 us -> 117 us  [the longest x1 115 us: whole_step(): pl.pallas_call(kernel, in_specs=[VMEM] * 14, out_specs=[VMEM] * 4, out_sh...]
where the time goes in v3:
time: 119 us
  Pallas kernels  117 us (98%)
  local copies, waits for them, and re-layouts  1.26 us (1%)
    pallas_call x1, Pallas kernels, whole_step(): pl.pallas_call(kernel, in_specs=[VMEM] * 14, out_specs=[VMEM] * 4, out_sh...  115 us

profile of v3, /device:TPU:1, one launch (start us, length us, event | category | flops | bytes accessed | tf_op | source)
XLA Modules:
  0.0 119.3 jit_solution(15231459064879152318)
XLA Ops:
  0.6 0.0 copy-start
  0.7 0.7 copy-done
  1.3 0.6 reshape.49.rmask
  1.9 115.1 %whole_step.1 = (bf16[48,48,128]{2,1,0:T(8,128)(2,1)}, bf16[16,32,128]{2,1,0:T(8,128)(2,1)}, bf16[16,16,128]{2,1,0:T(8,128)(2,1)}, f32[16,128]{1,0:T(8,128)}) custom-call(bf16[48,48,128]{2,1,0:T(8,128)(2,1)} %pm.1, bf16[48,48,128]{2,1,0:T(8,128)(2,1)} %sp.1, bf16[48,48,128]{2,1,0:T(8,128)(2,1)} %ct.1, s32[1,768]{1,0:T(1,128)} %reshape.49.rmask, ...), custom_call_target="tpu_custom_call" | custom-call | tf_op jit(solution)/shard_map/whole_step/pallas_call | solution.py:431
  117.1 2.1 %finish.1 = (bf16[48,48,128]{2,1,0:T(8,128)(2,1)}, f32[128,128]{1,0:T(8,128)}, f32[128,128]{1,0:T(8,128)}, f32[128,128]{1,0:T(8,128)}, f32[128,128]{1,0:T(8,128)...) custom-call(bf16[48,48,128]{2,1,0:T(8,128)(2,1)} %get-tuple-element., ...), custom_call_target="tpu_custom_call" | custom-call | tf_op jit(solution)/shard_map/finish/pallas_call | solution.py:519
Async XLA Ops:
  0.6 0.7 copy-start

commit v4 on v3

--- a/solution.py
+++ b/solution.py
@@ -16,23 +16,21 @@
 BLK = 48
 CH = 128
 PACK = 8
-GROUPS = BLK // PACK
 LANES = PACK * BLK
 TILES = LANES // 128
-CPD = CH // DEV
-ROWS = GROUPS * CPD
-CROWS = GROUPS * DEV
+ZN = 8
+PLANE = 32
+CPZ = CH // ZN
 N = DEV * BLK
 STEP = 16
 CELLS = STEP * BLK
 NSTEP = BLK // STEP
 EARLY = 4 * CH // DEV
 LATE = 2 * CH // DEV
-PROWS = STEP // PACK * CPD
-CPROWS = STEP // PACK * DEV
+PROWS = STEP // PACK * CPZ
+CPROWS = STEP // PACK * ZN
 PN = STEP * DEV
 NT = N // 128
-ODD = 11
 
 
 def dot(a, b, ca=1, cb=0):
@@ -58,7 +56,7 @@
     halves = []
     for g in range(STEP // PACK):
         turned = values[g * LANES : (g + 1) * LANES].T
-        halves.append(turned.reshape(DEV, CPD, LANES))
+        halves.append(turned.reshape(ZN, CPZ, LANES))
     ref[...] = jnp.concatenate(halves, axis=1).astype(bf16)
 
 
@@ -66,7 +64,7 @@
     values = ref[...].astype(f32)
     parts = []
     for g in range(STEP // PACK):
-        parts.append(values[:, g * CPD : (g + 1) * CPD, :].reshape(CH, LANES).T)
+        parts.append(values[:, g * CPZ : (g + 1) * CPZ, :].reshape(CH, LANES).T)
     return jnp.concatenate(parts, axis=0)
 
 
@@ -83,9 +81,12 @@
 
 def mask_of(rmask, axis):
     first = lax.axis_index(axis) * BLK
-    lane = lax.broadcasted_iota(jnp.int32, (BLK, N), 1)
-    sub = lax.broadcasted_iota(jnp.int32, (BLK, N), 0)
-    picked = jnp.where(lane == sub + first, rmask[...].astype(f32), 0.0)
+    lane = lax.broadcasted_iota(jnp.int32, (BLK, CH), 1)
+    sub = lax.broadcasted_iota(jnp.int32, (BLK, CH), 0)
+    picked = jnp.zeros((BLK, CH), f32)
+    for t in range(NT):
+        here = lane + t * CH == sub + first
+        picked += jnp.where(here, rmask[t : t + 1, :].astype(f32), 0.0)
     return jnp.broadcast_to(jnp.sum(picked, axis=1, keepdims=True), (BLK, CH))
 
 
@@ -105,19 +106,33 @@
     pltpu.make_async_copy(ref, ref, sem).wait()
 
 
-def push(src, dst, send, recv, axis, t):
+def push(src, dst, send, recv, where):
     pltpu.make_async_remote_copy(
         src_ref=src,
         dst_ref=dst,
         send_sem=send,
         recv_sem=recv,
-        device_id={axis: t},
+        device_id=where,
         device_id_type=MESH,
     ).start()
 
 
 def keep(src, dst, sem):
     pltpu.make_async_copy(src, dst, sem).start()
+
+
+def scatter_z(src, dst, send, recv):
+    row = lax.axis_index("row")
+    z = row >> 1
+    keep(src(z), dst.at[z], recv)
+
+    def go(d):
+        k = ZN - d
+        away = jnp.where((k & 1) == 1, (k + 1) >> 1, ZN - (k >> 1))
+        t = (z + away) & (ZN - 1)
+        push(src(t), dst.at[z], send, recv, {"row": 2 * t + (row & 1)})
+
+    span(ZN, go, 1)
 
 
 def scatter(axis, src, dst, send, recv):
@@ -125,19 +140,22 @@
     keep(src(me), dst.at[me], recv)
 
     def go(d):
-        t = peer(axis, (d * ODD) & (DEV - 1))
-        push(src(t), dst.at[me], send, recv, axis, t)
+        t = peer(axis, DEV - d)
+        push(src(t), dst.at[me], send, recv, {axis: t})
 
     span(DEV, go, 1)
 
 
-def assemble(src, scr, dst, first):
-    for a in range(PACK):
-        rows = jnp.concatenate(
-            [src[q][:, a * BLK : (a + 1) * BLK].astype(f32) for q in range(DEV)], axis=1
-        )
-        for t in range(NT):
-            scr[t, pl.ds(a, CPROWS, stride=PACK), :] = rows[:, t * 128 : (t + 1) * 128]
+def assemble(pick, scr, dst, first):
+    for y in range(2):
+        for a in range(PACK):
+            rows = jnp.concatenate(
+                [pick(y, q)[:, a * BLK : (a + 1) * BLK].astype(f32) for q in range(DEV)], axis=1
+            )
+            for t in range(NT):
+                scr[t, pl.ds(y * (PN // 2) + a, CPROWS, stride=PACK), :] = rows[
+                    :, t * 128 : (t + 1) * 128
+                ]
     for t in range(NT):
         dst[first : first + PN, t * 128 : (t + 1) * 128] = scr[t].astype(bf16)
 
@@ -146,22 +164,35 @@
     lane = lax.broadcasted_iota(jnp.int32, (N, N), 1)
     sub = lax.broadcasted_iota(jnp.int32, (N, N), 0)
     piece = lane >> 8
-    place = ((lane >> 4) & 15) * BLK + piece * STEP + (lane & 15)
+    device = 2 * ((lane >> 4) & 7) + ((lane >> 7) & 1)
+    place = device * BLK + piece * STEP + (lane & 15)
     return jnp.where(place == sub, 1.0, 0.0).astype(bf16)
 
 
 def kernel(
-    pm, sp, ct, rmask, lg, lb, og, ob, wa, wag, wb, wbg, wg, wo,
-    gp, eout, lout, vout,
-    zn, hat, inv, a1, a2, b1, b2, gg, gz, gwo, gwa, gwb, lvec, wcat, tx, rx,
-    rbuf, scr, sbuf, gq, fq, asm, gn, left, order, fn, acc, dis, cbuf, hbuf,
-    epart, eg1, emid, eg2, efin, lpart, lg1, lmid, lg2, lfin,
-    r_send, r_recv, g_send, g_recv, x_send, x_recv, f_send, f_recv,
-    c_send, c_recv, h_send, h_recv, e_send, e_recv, l_send, l_recv,
+    *refs
 ):
+    given, refs = refs[:14], refs[14:]
+    (
+        gp, eout, lout, vout,
+        zn, hat, inv, a1, a2, b1, b2, gg, gz, gwo, gwa, gwb, lvec, wcat, tx, rx,
+        rbuf, scr, sbuf, gq, fq, asm, gn, left, order, fn, acc, dis, cbuf, hbuf,
+        epart, eg1, emid, eg2, efin, lpart, lg1, lmid, lg2, lfin,
+        r_send, r_recv, g_send, g_recv, x_send, x_recv, f_send, f_recv,
+        c_send, c_recv, h_send, h_recv, e_send, e_recv, l_send, l_recv, i_recv,
+        *held
+    ) = refs
+    (
+        pm, sp, ct, rmask, lg, lb, og, ob, wa, wag, wb, wbg, wg, wo,
+    ) = held
     row, col = lax.axis_index("row"), lax.axis_index("col")
-    odd = lax.rem(col, 2)
-    sibling = col + 1 - 2 * odd
+    odd = col & 1
+    place = (row & 1) * DEV + col
+    chip = place >> 1
+
+    def at_place(t):
+        return {"row": row - (row & 1) + (t >> 4), "col": t & (DEV - 1)}
+
     barrier = pltpu.get_barrier_semaphore()
     for axis in ("row", "col"):
 
@@ -172,7 +203,18 @@
 
         span(DEV, hello, 1)
 
+    def hello_plane(d):
+        pl.semaphore_signal(
+            barrier, inc=1, device_id={"row": row ^ 1, "col": col ^ d}, device_id_type=MESH
+        )
+
+    span(DEV, hello_plane, 1)
+
+    for k in range(14):
+        keep(given[k], held[k], i_recv.at[k])
     lvec[...] = jnp.zeros((8, CH), f32)
+    for k in range(14):
+        arrive(held[k], i_recv.at[k])
     rm = mask_of(rmask, "row")
     km = mask_of(rmask, "col")
     for k, w in enumerate((wa, wag, wg, wb, wbg)):
@@ -185,7 +227,7 @@
         return slice(p * STEP, (p + 1) * STEP)
 
     def launch(a, p):
-        scatter("row", lambda t: tx.at[a, p, t], rbuf.at[a, p], r_send.at[a], r_recv.at[a, p])
+        scatter_z(lambda t: tx.at[a, p, t], rbuf.at[a, p], r_send.at[a], r_recv.at[a, p])
 
     for p in range(NSTEP):
         here = cells(p)
@@ -202,7 +244,7 @@
         gxn = dot(gu, wo[...], 1, 1)
         to_channels(tx.at[0, p], norm_back(gxn * og[...], ohat, oinv))
         if p == 0:
-            pl.semaphore_wait(barrier, 2 * (DEV - 1))
+            pl.semaphore_wait(barrier, 3 * (DEV - 1))
         launch(0, p)
         update = dot(xn, wo[...])
         gg[here] = (up * update * (1.0 - gate)).astype(bf16)
@@ -229,56 +271,68 @@
         arrive(rbuf.at[a, p], r_recv.at[a, p])
         for t in range(TILES):
             lanes = slice(t * 128, (t + 1) * 128)
-            scr[t] = rbuf[a, p, :, :, lanes].reshape(DEV * PROWS, 128).astype(f32)
-            for m in range(CPD):
-                sbuf[a, p, m, :, lanes] = scr[t, pl.ds(m, CPROWS, stride=CPD), :].astype(bf16)
-
-    HALF = CPROWS // 2
-
-    def half(h):
-        return pl.ds(pl.multiple_of(h * HALF, HALF), HALF)
-
-    for p in range(NSTEP):
+            scr[t] = rbuf[a, p, :, :, lanes].reshape(ZN * PROWS, 128).astype(f32)
+            for m in range(CPZ):
+                sbuf[a, p, m, :, lanes] = scr[t, pl.ds(m, CPROWS, stride=CPZ), :].astype(bf16)
+
+    def divide(p):
         shuffle(0, p)
-        keep(sbuf.at[0, p, col // 2, half(odd)], gq.at[p, col, half(odd)], g_recv.at[p])
-
-        def send(d, p=p):
-            t = peer("col", (d * ODD) & (DEV - 1))
-            h = half(lax.rem(t, 2))
-            push(sbuf.at[0, p, t // 2, h], gq.at[p, col, h], g_send, g_recv.at[p], "col", t)
+        keep(sbuf.at[0, p, chip], gq.at[p, odd, chip], g_recv.at[p])
+
+        def send(d):
+            t = chip ^ (DEV - d)
+            push(
+                sbuf.at[0, p, t], gq.at[p, odd, chip], g_send, g_recv.at[p], at_place(2 * t + odd)
+            )
 
         span(DEV, send, 1)
+
+    def exchange(p):
+        mine = gq.at[p, odd]
+        arrive(mine, g_recv.at[p])
+        push(mine, mine, x_send.at[p], x_recv.at[p], {"col": col ^ 1})
+
+    def gather(p):
+        arrive(gq.at[p, 1 - odd], x_recv.at[p])
+        assemble(lambda y, q: gq[p, q % 2, (y * DEV + q) // 2], asm, gn, p * PN)
 
     def factor(a, p):
         shuffle(a, p)
         same = odd == a - 1
 
+        def send(d):
+            t = chip ^ (DEV - d)
+            push(
+                sbuf.at[a, p, t],
+                fq.at[p, place],
+                f_send,
+                f_recv.at[p],
+                at_place(2 * t + a - 1),
+            )
+
+        span(DEV, send, 1)
+
         @pl.when(same)
         def _():
-            keep(sbuf.at[a, p, col // 2], fq.at[p, col], f_recv.at[p])
-
-        def send(d):
-            t = col ^ (2 * ((d * ODD) & (DEV // 2 - 1)) + jnp.where(same, 0, 1))
-            push(sbuf.at[a, p, t // 2], fq.at[p, col], f_send, f_recv.at[p], "col", t)
-
-        span(DEV // 2, send, jnp.where(same, 1, 0))
-
+            keep(sbuf.at[a, p, chip], fq.at[p, place], f_recv.at[p])
+
+        @pl.when(jnp.logical_not(same))
+        def _():
+            push(
+                sbuf.at[a, p, chip], fq.at[p, place], f_send, f_recv.at[p], {"col": col ^ 1}
+            )
+
+    divide(0)
+    divide(1)
+    exchange(0)
+    divide(2)
+    exchange(1)
     factor(1, 0)
-    for p in range(NSTEP):
-        arrive(gq.at[p, :, half(odd)], g_recv.at[p])
-        push(
-            gq.at[p, :, half(odd)],
-            gq.at[p, :, half(odd)],
-            x_send.at[p],
-            x_recv.at[p],
-            "col",
-            sibling,
-        )
+    gather(0)
+    exchange(2)
+    gather(1)
     factor(1, 1)
-    factor(1, 2)
-    for p in range(NSTEP):
-        arrive(gq.at[p, :, half(1 - odd)], x_recv.at[p])
-        assemble(gq.at[p], asm, gn, p * PN)
+    gather(2)
 
     @pl.when(odd == 0)
     def _():
@@ -288,56 +342,95 @@
     def _():
         left[...] = dot(order[...], gn[...], 0, 1).astype(bf16)
 
-    factor(2, 0)
-
-    def multiply():
+    factor(1, 2)
+
+    def multiply(p):
+        arrive(fq.at[p], f_recv.at[p])
+        assemble(lambda y, q: fq[p, y * DEV + q], asm, fn, 0)
+        values = dot(left[:, p * PN : (p + 1) * PN], fn[...])
+        for t in range(NT):
+            add_to(acc.at[t], values[:, t * 128 : (t + 1) * 128], p == 0)
+
+    def give_back():
         for p in range(NSTEP):
-            arrive(fq.at[p], f_recv.at[p])
-            assemble(fq.at[p], asm, fn, 0)
-            values = dot(left[:, p * PN : (p + 1) * PN], fn[...])
-            for t in range(NT):
-                lanes = values[:, t * 128 : (t + 1) * 128]
-                if p == 0:
-                    acc[t] = lanes
-                else:
-                    acc[t] += lanes
-        for p in range(NSTEP):
-            rows = [
-                [acc[t, pl.ds(p * PN + a, CPROWS, stride=PACK), :] for t in range(NT)]
-                for a in range(PACK)
-            ]
-
-            def piece(a, q):
-                lo, hi = q * BLK, (q + 1) * BLK
-                first, last = lo // 128, (hi - 1) // 128
-                if first == last:
-                    return rows[a][first][:, lo - first * 128 : hi - first * 128]
-                return jnp.concatenate(
-                    [rows[a][first][:, lo - first * 128 :], rows[a][last][:, : hi - last * 128]],
-                    axis=1,
+            for y in range(2):
+                base = p * PN + y * (PN // 2)
+                rows = [
+                    [acc[t, pl.ds(base + a, CPROWS, stride=PACK), :] for t in range(NT)]
+                    for a in range(PACK)
+                ]
+
+                def piece(a, q, rows=rows):
+                    lo, hi = q * BLK, (q + 1) * BLK
+                    first, last = lo // 128, (hi - 1) // 128
+                    if first == last:
+                        return rows[a][first][:, lo - first * 128 : hi - first * 128]
+                    return jnp.concatenate(
+                        [
+                            rows[a][first][:, lo - first * 128 :],
+                            rows[a][last][:, : hi - last * 128],
+                        ],
+                        axis=1,
+                    )
+
+                for q in range(DEV):
+                    dis[p, y * DEV + q] = jnp.concatenate(
+                        [piece(a, q) for a in range(PACK)], axis=1
+                    ).astype(bf16)
+            keep(dis.at[p, place], cbuf.at[p, place], c_recv.at[odd, p])
+
+            def send(d, p=p):
+                t = place ^ (PLANE - d)
+                push(
+                    dis.at[p, t], cbuf.at[p, place], c_send, c_recv.at[odd, p], at_place(t)
                 )
 
-            for q in range(DEV):
-                dis[p, q] = jnp.concatenate([piece(a, q) for a in range(PACK)], axis=1).astype(bf16)
-            scatter("col", lambda t: dis.at[p, t], cbuf.at[p], c_send, c_recv.at[odd, p])
-
-    pl.when(odd == 0)(multiply)
-    factor(2, 1)
-    factor(2, 2)
-    pl.when(odd == 1)(multiply)
+            span(PLANE, send, 1)
 
     def relay(h, p):
-        arrive(cbuf.at[p, 0 : DEV // 2], c_recv.at[h, p])
+        arrive(cbuf.at[p, 0 : PLANE // 2], c_recv.at[h, p])
         for t in range(TILES):
             lanes = slice(t * 128, (t + 1) * 128)
-            for m in range(CPD):
-                scr[t, pl.ds(m, CPROWS, stride=CPD), :] = cbuf[p, 2 * m + h, :, lanes].astype(f32)
-            hbuf[h, p, :, :, lanes] = scr[t].reshape(DEV, PROWS, 128).astype(bf16)
-        scatter("row", lambda t: hbuf.at[h, p, t], rx.at[h, p], h_send, h_recv.at[h, p])
-
-    for h in range(2):
-        for p in range(NSTEP):
-            relay(h, p)
+            for m in range(CPZ):
+                scr[t, pl.ds(m, CPROWS, stride=CPZ), :] = cbuf[p, 2 * m + h, :, lanes].astype(f32)
+            hbuf[h, p, :, :, lanes] = scr[t].reshape(ZN, PROWS, 128).astype(bf16)
+        scatter_z(lambda t: hbuf.at[h, p, t], rx.at[h, p], h_send, h_recv.at[h, p])
+
+    @pl.when(odd == 0)
+    def _():
+        multiply(0)
+        multiply(1)
+
+    factor(2, 0)
+
+    @pl.when(odd == 0)
+    def _():
+        multiply(2)
+        give_back()
+
+    factor(2, 1)
+
+    @pl.when(odd == 1)
+    def _():
+        multiply(0)
+
+    relay(0, 0)
+    factor(2, 2)
+
+    @pl.when(odd == 1)
+    def _():
+        multiply(1)
+
+    relay(0, 1)
+    relay(0, 2)
+
+    @pl.when(odd == 1)
+    def _():
+        multiply(2)
+        give_back()
+
+    for p in range(NSTEP):
+        relay(1, p)
 
     def grads_of(h, p, k1, k2):
         arrive(rx.at[h, p], h_recv.at[h, p])
@@ -372,13 +465,7 @@
         gp[rows_of(p)] = value.astype(bf16).reshape(STEP, BLK, CH)
 
     write(0, last(0))
-    arrive(eg1, e_recv.at[0])
-    emid[...] = jnp.sum(eg1[...].astype(f32), axis=0).astype(bf16)
-    scatter("row", lambda t: emid, eg2, e_send.at[1], e_recv.at[1])
     write(1, last(1))
-    arrive(eg2, e_recv.at[1])
-    efin[...] = (jnp.sum(eg2[...].astype(f32), axis=0) * (1.0 / N)).astype(bf16)
-    scatter("col", lambda t: efin, eout, e_send.at[2], e_recv.at[2])
     total = last(2)
 
     vector = jnp.concatenate([lvec[...], jnp.zeros((8, CH), f32)], axis=0)
@@ -387,10 +474,16 @@
         source = gwb[at : at + LATE, k * CH : (k + 1) * CH]
         lpart[t] = jnp.concatenate([source, vector], axis=0).astype(bf16)
     scatter("col", lambda t: lpart.at[t], lg1, l_send.at[0], l_recv.at[0])
+    arrive(eg1, e_recv.at[0])
+    emid[...] = jnp.sum(eg1[...].astype(f32), axis=0).astype(bf16)
+    scatter("row", lambda t: emid, eg2, e_send.at[1], e_recv.at[1])
     write(2, total)
     arrive(lg1, l_recv.at[0])
     lmid[...] = jnp.sum(lg1[...].astype(f32), axis=0).astype(bf16)
     scatter("row", lambda t: lmid, lg2, l_send.at[1], l_recv.at[1])
+    arrive(eg2, e_recv.at[1])
+    efin[...] = (jnp.sum(eg2[...].astype(f32), axis=0) * (1.0 / N)).astype(bf16)
+    scatter("col", lambda t: efin, eout, e_send.at[2], e_recv.at[2])
     arrive(lg2, l_recv.at[1])
     done = jnp.sum(lg2[...].astype(f32), axis=0) * (1.0 / N)
     vout[...] = done[LATE:]
@@ -398,13 +491,13 @@
     scatter("col", lambda t: lfin, lout, l_send.at[2], l_recv.at[2])
 
     for a in range(3):
-        arrive(rbuf.at[a, :, 0 : DEV - 1], r_send.at[a])
-    arrive(gq.at[:, 0 : DEV - 1, 0:HALF], g_send)
+        arrive(rbuf.at[a, :, 0 : ZN - 1], r_send.at[a])
+    arrive(gq.at[:, 0, 0 : DEV - 1], g_send)
     for p in range(NSTEP):
-        arrive(gq.at[p, :, 0:HALF], x_send.at[p])
-    arrive(fq.at[:, 0 : DEV - 1], f_send)
-    arrive(cbuf.at[:, 0 : DEV - 1], c_send)
-    arrive(hbuf.at[:, :, 0 : DEV - 1], h_send)
+        arrive(gq.at[p, 0], x_send.at[p])
+    arrive(fq.at[:, 0 : PLANE - 1], f_send)
+    arrive(cbuf.at[:, 0 : PLANE - 1], c_send)
+    arrive(hbuf.at[:, :, 0 : ZN - 1], h_send)
     for k in range(3):
         arrive(eg1.at[0 : DEV - 1], e_send.at[k])
     arrive(lg1.at[0 : DEV - 1], l_send.at[0])
@@ -416,8 +509,8 @@
 
 def whole_step(*args):
     dma = pltpu.SemaphoreType.DMA
-    turned = (NSTEP, DEV, PROWS, LANES)
-    crossed = (NSTEP, DEV, CPROWS, LANES)
+    turned = (NSTEP, ZN, PROWS, LANES)
+    crossed = (NSTEP, PLANE, CPROWS, LANES)
     flat = (BLK * BLK, CH)
     early = (DEV, EARLY, CH)
     late = (DEV, LATE + 16, CH)
@@ -430,7 +523,7 @@
 
     return pl.pallas_call(
         kernel,
-        in_specs=[VMEM] * 14,
+        in_specs=[pl.BlockSpec(memory_space=pl.ANY)] * 14,
         out_specs=[VMEM] * 4,
         out_shape=[
             jax.ShapeDtypeStruct((BLK, BLK, CH), bf16),
@@ -456,9 +549,9 @@
             thin(3, *turned),
             thin(2, *turned),
             thin(3, *turned),
-            wide(TILES, DEV * PROWS, 128),
-            thin(3, NSTEP, CPD, CPROWS, LANES),
-            thin(*crossed),
+            wide(TILES, ZN * PROWS, 128),
+            thin(3, NSTEP, CPZ, CPROWS, LANES),
+            thin(NSTEP, 2, DEV, CPROWS, LANES),
             thin(*crossed),
             wide(NT, PN, 128),
             thin(N, N),
@@ -495,7 +588,9 @@
             dma((3,)),
             dma((3,)),
             dma((3,)),
-        ],
+            dma((14,)),
+        ]
+        + [pltpu.VMEM(a.shape, a.dtype) for a in args],
         name="whole_step",
         compiler_params=pltpu.CompilerParams(
             collective_id=1, has_side_effects=True, vmem_limit_bytes=LIMIT
@@ -541,7 +636,7 @@
     vecs = [v.reshape(1, CH) for v in (ln_gain, ln_bias, out_gain, out_bias)]
     outs = finish(
         *whole_step(
-            pair_map, saved_product, cotangent, residue_mask.reshape(1, N), *vecs, *weights
+            pair_map, saved_product, cotangent, residue_mask.reshape(NT, CH), *vecs, *weights
         )
     )
     return tuple(outs[:7]) + tuple(v.reshape(CH) for v in outs[7:])

time: 119 us -> 105 us (0.88)
  Pallas kernels: 117 us -> 104 us
  local copies, waits for them, and re-layouts: 1.26 us -> 0 us
    pallas_call x1, Pallas kernels: 115 us -> 102 us  [whole_step(): pl.pallas_call(kernel, in_specs=[pl.BlockSpec(memory_space=pl.ANY)] * 14,...]
where the time goes in v4:
time: 105 us
  Pallas kernels  104 us (99%)
    pallas_call x1, Pallas kernels, whole_step(): pl.pallas_call(kernel, in_specs=[pl.BlockSpec(memory_space=pl.ANY)] * 14,...  102 us
    pallas_call x1, Pallas kernels, finish(): pl.pallas_call(finish_kernel, in_specs=[VMEM] * 4, out_specs=[VMEM] * 11,...  2.11 us

profile of v4, /device:TPU:1, one launch (start us, length us, event | category | flops | bytes accessed | tf_op | source)
XLA Modules:
  0.0 104.9 jit_solution(11367696436764586897)
XLA Ops:
  0.6 102.0 %whole_step.1 = (bf16[48,48,128]{2,1,0:T(8,128)(2,1)}, bf16[16,32,128]{2,1,0:T(8,128)(2,1)}, bf16[16,16,128]{2,1,0:T(8,128)(2,1)}, f32[16,128]{1,0:T(8,128)}) custom-call(bf16[48,48,128]{2,1,0:T(8,128)(2,1)} %refs_0_.1, bf16[48,48,128]{2,1,0:T(8,128)(2,1)} %refs_1_.1, bf16[48,48,128]{2,1,0:T(8,128)(2,1)} %refs_2_.1, s32[6,128]{1,0:T(8,128)} %bitcast.9, ...), custom_call_target="tpu_custom_call" | custom-call | tf_op jit(solution)/shard_map/whole_step/pallas_call | solution.py:524
  102.6 2.1 %finish.1 = (bf16[48,48,128]{2,1,0:T(8,128)(2,1)}, f32[128,128]{1,0:T(8,128)}, f32[128,128]{1,0:T(8,128)}, f32[128,128]{1,0:T(8,128)}, f32[128,128]{1,0:T(8,128)...) custom-call(bf16[48,48,128]{2,1,0:T(8,128)(2,1)} %get-tuple-element., ...), custom_call_target="tpu_custom_call" | custom-call | tf_op jit(solution)/shard_map/finish/pallas_call | solution.py:614

commit v5 on v4

--- a/solution.py
+++ b/solution.py
@@ -19,7 +19,7 @@
 LANES = PACK * BLK
 TILES = LANES // 128
 ZN = 8
-PLANE = 32
+HALF = DEV // 2
 CPZ = CH // ZN
 N = DEV * BLK
 STEP = 16
@@ -146,17 +146,18 @@
     span(DEV, go, 1)
 
 
-def assemble(pick, scr, dst, first):
+def assemble(pick, count, scr, dst, first):
+    tiles = count * BLK // 128
     for y in range(2):
         for a in range(PACK):
             rows = jnp.concatenate(
-                [pick(y, q)[:, a * BLK : (a + 1) * BLK].astype(f32) for q in range(DEV)], axis=1
+                [pick(y, q)[:, a * BLK : (a + 1) * BLK].astype(f32) for q in range(count)], axis=1
             )
-            for t in range(NT):
+            for t in range(tiles):
                 scr[t, pl.ds(y * (PN // 2) + a, CPROWS, stride=PACK), :] = rows[
                     :, t * 128 : (t + 1) * 128
                 ]
-    for t in range(NT):
+    for t in range(tiles):
         dst[first : first + PN, t * 128 : (t + 1) * 128] = scr[t].astype(bf16)
 
 
@@ -176,7 +177,7 @@
     (
         gp, eout, lout, vout,
         zn, hat, inv, a1, a2, b1, b2, gg, gz, gwo, gwa, gwb, lvec, wcat, tx, rx,
-        rbuf, scr, sbuf, gq, fq, asm, gn, left, order, fn, acc, dis, cbuf, hbuf,
+        rbuf, scr, sbuf, gq, fq, asm, gn, left, below, order, fn, acc, dis, cbuf, hbuf,
         epart, eg1, emid, eg2, efin, lpart, lg1, lmid, lg2, lfin,
         r_send, r_recv, g_send, g_recv, x_send, x_recv, f_send, f_recv,
         c_send, c_recv, h_send, h_recv, e_send, e_recv, l_send, l_recv, i_recv,
@@ -294,33 +295,20 @@
 
     def gather(p):
         arrive(gq.at[p, 1 - odd], x_recv.at[p])
-        assemble(lambda y, q: gq[p, q % 2, (y * DEV + q) // 2], asm, gn, p * PN)
+        assemble(lambda y, q: gq[p, q % 2, (y * DEV + q) // 2], DEV, asm, gn, p * PN)
 
     def factor(a, p):
         shuffle(a, p)
-        same = odd == a - 1
+        h = a - 1
+        keep(sbuf.at[a, p, chip], fq.at[h, p, chip], f_recv.at[h, p])
 
         def send(d):
             t = chip ^ (DEV - d)
             push(
-                sbuf.at[a, p, t],
-                fq.at[p, place],
-                f_send,
-                f_recv.at[p],
-                at_place(2 * t + a - 1),
+                sbuf.at[a, p, t], fq.at[h, p, chip], f_send, f_recv.at[h, p], at_place(2 * t + odd)
             )
 
         span(DEV, send, 1)
-
-        @pl.when(same)
-        def _():
-            keep(sbuf.at[a, p, chip], fq.at[p, place], f_recv.at[p])
-
-        @pl.when(jnp.logical_not(same))
-        def _():
-            push(
-                sbuf.at[a, p, chip], fq.at[p, place], f_send, f_recv.at[p], {"col": col ^ 1}
-            )
 
     divide(0)
     divide(1)
@@ -334,34 +322,28 @@
     factor(1, 1)
     gather(2)
 
-    @pl.when(odd == 0)
-    def _():
-        left[...] = dot(gn[...], order[...]).astype(bf16)
-
-    @pl.when(odd == 1)
-    def _():
-        left[...] = dot(order[...], gn[...], 0, 1).astype(bf16)
-
+    left[...] = dot(gn[...], order[...]).astype(bf16)
     factor(1, 2)
 
-    def multiply(p):
-        arrive(fq.at[p], f_recv.at[p])
-        assemble(lambda y, q: fq[p, y * DEV + q], asm, fn, 0)
-        values = dot(left[:, p * PN : (p + 1) * PN], fn[...])
-        for t in range(NT):
+    def multiply(h, p):
+        arrive(fq.at[h, p], f_recv.at[h, p])
+        assemble(lambda y, j: fq[h, p, y * HALF + j], HALF, asm, fn, 0)
+        sides = (left, below)[h]
+        values = dot(sides[:, p * PN : (p + 1) * PN], fn[...])
+        for t in range(NT // 2):
             add_to(acc.at[t], values[:, t * 128 : (t + 1) * 128], p == 0)
 
-    def give_back():
+    def give_back(h):
         for p in range(NSTEP):
             for y in range(2):
                 base = p * PN + y * (PN // 2)
                 rows = [
-                    [acc[t, pl.ds(base + a, CPROWS, stride=PACK), :] for t in range(NT)]
+                    [acc[t, pl.ds(base + a, CPROWS, stride=PACK), :] for t in range(NT // 2)]
                     for a in range(PACK)
                 ]
 
-                def piece(a, q, rows=rows):
-                    lo, hi = q * BLK, (q + 1) * BLK
+                def piece(a, j, rows=rows):
+                    lo, hi = j * BLK, (j + 1) * BLK
                     first, last = lo // 128, (hi - 1) // 128
                     if first == last:
                         return rows[a][first][:, lo - first * 128 : hi - first * 128]
@@ -373,61 +355,48 @@
                         axis=1,
                     )
 
-                for q in range(DEV):
-                    dis[p, y * DEV + q] = jnp.concatenate(
-                        [piece(a, q) for a in range(PACK)], axis=1
+                for j in range(HALF):
+                    dis[h, p, y * HALF + j] = jnp.concatenate(
+                        [piece(a, j) for a in range(PACK)], axis=1
                     ).astype(bf16)
-            keep(dis.at[p, place], cbuf.at[p, place], c_recv.at[odd, p])
+            keep(dis.at[h, p, chip], cbuf.at[h, p, chip], c_recv.at[h, p])
 
             def send(d, p=p):
-                t = place ^ (PLANE - d)
+                t = chip ^ (DEV - d)
                 push(
-                    dis.at[p, t], cbuf.at[p, place], c_send, c_recv.at[odd, p], at_place(t)
+                    dis.at[h, p, t],
+                    cbuf.at[h, p, chip],
+                    c_send,
+                    c_recv.at[h, p],
+                    at_place(2 * t + odd),
                 )
 
-            span(PLANE, send, 1)
+            span(DEV, send, 1)
 
     def relay(h, p):
-        arrive(cbuf.at[p, 0 : PLANE // 2], c_recv.at[h, p])
+        arrive(cbuf.at[h, p], c_recv.at[h, p])
         for t in range(TILES):
             lanes = slice(t * 128, (t + 1) * 128)
             for m in range(CPZ):
-                scr[t, pl.ds(m, CPROWS, stride=CPZ), :] = cbuf[p, 2 * m + h, :, lanes].astype(f32)
+                scr[t, pl.ds(m, CPROWS, stride=CPZ), :] = cbuf[h, p, m, :, lanes].astype(f32)
             hbuf[h, p, :, :, lanes] = scr[t].reshape(ZN, PROWS, 128).astype(bf16)
         scatter_z(lambda t: hbuf.at[h, p, t], rx.at[h, p], h_send, h_recv.at[h, p])
 
-    @pl.when(odd == 0)
-    def _():
-        multiply(0)
-        multiply(1)
-
+    multiply(0, 0)
+    multiply(0, 1)
+    multiply(0, 2)
+    give_back(0)
     factor(2, 0)
-
-    @pl.when(odd == 0)
-    def _():
-        multiply(2)
-        give_back()
-
+    below[...] = dot(order[...], gn[...], 0, 1).astype(bf16)
     factor(2, 1)
-
-    @pl.when(odd == 1)
-    def _():
-        multiply(0)
-
     relay(0, 0)
+    multiply(1, 0)
     factor(2, 2)
-
-    @pl.when(odd == 1)
-    def _():
-        multiply(1)
-
     relay(0, 1)
+    multiply(1, 1)
     relay(0, 2)
-
-    @pl.when(odd == 1)
-    def _():
-        multiply(2)
-        give_back()
+    multiply(1, 2)
+    give_back(1)
 
     for p in range(NSTEP):
         relay(1, p)
@@ -495,8 +464,8 @@
     arrive(gq.at[:, 0, 0 : DEV - 1], g_send)
     for p in range(NSTEP):
         arrive(gq.at[p, 0], x_send.at[p])
-    arrive(fq.at[:, 0 : PLANE - 1], f_send)
-    arrive(cbuf.at[:, 0 : PLANE - 1], c_send)
+    arrive(fq.at[:, :, 0 : DEV - 1], f_send)
+    arrive(cbuf.at[:, :, 0 : DEV - 1], c_send)
     arrive(hbuf.at[:, :, 0 : ZN - 1], h_send)
     for k in range(3):
         arrive(eg1.at[0 : DEV - 1], e_send.at[k])
@@ -510,7 +479,7 @@
 def whole_step(*args):
     dma = pltpu.SemaphoreType.DMA
     turned = (NSTEP, ZN, PROWS, LANES)
-    crossed = (NSTEP, PLANE, CPROWS, LANES)
+    crossed = (2, NSTEP, DEV, CPROWS, LANES)
     flat = (BLK * BLK, CH)
     early = (DEV, EARLY, CH)
     late = (DEV, LATE + 16, CH)
@@ -557,8 +526,9 @@
             thin(N, N),
             thin(N, N),
             thin(N, N),
-            thin(PN, N),
-            wide(NT, N, 128),
+            thin(N, N),
+            thin(PN, N // 2),
+            wide(NT // 2, N, 128),
             thin(*crossed),
             thin(*crossed),
             thin(2, *turned),
@@ -579,7 +549,7 @@
             dma((NSTEP,)),
             dma((NSTEP,)),
             dma,
-            dma((NSTEP,)),
+            dma((2, NSTEP)),
             dma,
             dma((2, NSTEP)),
             dma,

time: 105 us -> 101 us (0.962)
  Pallas kernels: 104 us -> 99.6 us
    pallas_call x1, Pallas kernels: 102 us -> 97.5 us  [whole_step(): pl.pallas_call(kernel, in_specs=[pl.BlockSpec(memory_space=pl.ANY)] * 14,...]
where the time goes in v5:
time: 101 us; the launch traced here: 100 us
  Pallas kernels  99.6 us (99%)
    pallas_call x1, Pallas kernels, whole_step(): pl.pallas_call(kernel, in_specs=[pl.BlockSpec(memory_space=pl.ANY)] * 14,...  97.5 us
    pallas_call x1, Pallas kernels, finish(): pl.pallas_call(finish_kernel, in_specs=[VMEM] * 4, out_specs=[VMEM] * 11,...  2.11 us

profile of v5, /device:TPU:1, one launch (start us, length us, event | category | flops | bytes accessed | tf_op | source)
XLA Modules:
  0.0 100.4 jit_solution(15911587070296551779)
XLA Ops:
  0.6 97.5 %whole_step.1 = (bf16[48,48,128]{2,1,0:T(8,128)(2,1)}, bf16[16,32,128]{2,1,0:T(8,128)(2,1)}, bf16[16,16,128]{2,1,0:T(8,128)(2,1)}, f32[16,128]{1,0:T(8,128)}) custom-call(bf16[48,48,128]{2,1,0:T(8,128)(2,1)} %refs_0_.1, bf16[48,48,128]{2,1,0:T(8,128)(2,1)} %refs_1_.1, bf16[48,48,128]{2,1,0:T(8,128)(2,1)} %refs_2_.1, s32[6,128]{1,0:T(8,128)} %bitcast.9, ...), custom_call_target="tpu_custom_call" | custom-call | tf_op jit(solution)/shard_map/whole_step/pallas_call | solution.py:493
  98.1 2.1 %finish.1 = (bf16[48,48,128]{2,1,0:T(8,128)(2,1)}, f32[128,128]{1,0:T(8,128)}, f32[128,128]{1,0:T(8,128)}, f32[128,128]{1,0:T(8,128)}, f32[128,128]{1,0:T(8,128)...) custom-call(bf16[48,48,128]{2,1,0:T(8,128)(2,1)} %get-tuple-element., ...), custom_call_target="tpu_custom_call" | custom-call | tf_op jit(solution)/shard_map/finish/pallas_call | solution.py:584

commit v6 on v5

--- a/solution.py
+++ b/solution.py
@@ -384,9 +384,9 @@
 
     multiply(0, 0)
     multiply(0, 1)
+    factor(2, 0)
     multiply(0, 2)
     give_back(0)
-    factor(2, 0)
     below[...] = dot(order[...], gn[...], 0, 1).astype(bf16)
     factor(2, 1)
     relay(0, 0)

time: 101 us -> 98.9 us (0.979)
  Pallas kernels: 99.6 us -> 98 us
    pallas_call x1, Pallas kernels: 97.5 us -> 95.9 us  [whole_step(): pl.pallas_call(kernel, in_specs=[pl.BlockSpec(memory_space=pl.ANY)] * 14,...]
where the time goes in v6:
time: 98.9 us; the launch traced here: 98.8 us
  Pallas kernels  98 us (99%)
    pallas_call x1, Pallas kernels, whole_step(): pl.pallas_call(kernel, in_specs=[pl.BlockSpec(memory_space=pl.ANY)] * 14,...  95.9 us
    pallas_call x1, Pallas kernels, finish(): pl.pallas_call(finish_kernel, in_specs=[VMEM] * 4, out_specs=[VMEM] * 11,...  2.11 us

profile of v6, /device:TPU:1, one launch (start us, length us, event | category | flops | bytes accessed | tf_op | source)
XLA Modules:
  0.0 98.8 jit_solution(9285407369780749448)
XLA Ops:
  0.6 95.9 %whole_step.1 = (bf16[48,48,128]{2,1,0:T(8,128)(2,1)}, bf16[16,32,128]{2,1,0:T(8,128)(2,1)}, bf16[16,16,128]{2,1,0:T(8,128)(2,1)}, f32[16,128]{1,0:T(8,128)}) custom-call(bf16[48,48,128]{2,1,0:T(8,128)(2,1)} %refs_0_.1, bf16[48,48,128]{2,1,0:T(8,128)(2,1)} %refs_1_.1, bf16[48,48,128]{2,1,0:T(8,128)(2,1)} %refs_2_.1, s32[6,128]{1,0:T(8,128)} %bitcast.9, ...), custom_call_target="tpu_custom_call" | custom-call | tf_op jit(solution)/shard_map/whole_step/pallas_call | solution.py:493
  96.5 2.1 %finish.1 = (bf16[48,48,128]{2,1,0:T(8,128)(2,1)}, f32[128,128]{1,0:T(8,128)}, f32[128,128]{1,0:T(8,128)}, f32[128,128]{1,0:T(8,128)}, f32[128,128]{1,0:T(8,128)...) custom-call(bf16[48,48,128]{2,1,0:T(8,128)(2,1)} %get-tuple-element., ...), custom_call_target="tpu_custom_call" | custom-call | tf_op jit(solution)/shard_map/finish/pallas_call | solution.py:584
